TPU v7x, 32 devices: a whole 2x2x4 slice. The times are simulated.
32 devices in a mesh: ctx: 8 (over y, x, core), tp: 4 (over z).
Axes of the slice: x: 2, y: 2, z: 4, core: 2. Of those that a mesh axis runs over, the one named last changes fastest.
Arguments:
- tokens: bfloat16 [768, 4096], P(('ctx', 'tp')), may hold values from -6 to 6
- proj_weight: bfloat16 [4096, 3, 3072], P(None, None, 'tp'), may hold values from -0.09375 to 0.09375
- feat_taps: float32 [3, 3, 3072], P(None, None, 'tp'), may hold values from -2.5 to 2.5
- inner_taps: float32 [7, 3072], P(None, 'tp'), may hold values from -2.5 to 2.5
- grad_out: bfloat16 [768, 3072], P('ctx', 'tp'), may hold values from -6 to 6
Outputs:
- gated: bfloat16 [768, 3072], P('ctx', 'tp')
- grad_tokens: bfloat16 [768, 4096], P(('ctx', 'tp'))
All inputs are finite; a program needn't handle non-finite values.
Results may differ from a plain program's by a relative error of at most 0.025.
Values may be sent and summed in bfloat16 or wider, within the bound.
A program may use at most 64 MiB of HBM per device.

v0:
```python
import jax
import jax.numpy as jnp
from jax import lax
from jax.sharding import PartitionSpec as P


def from_behind(value, axis, steps):
    count = lax.axis_size(axis)
    first, last = (max(0, -steps), min(count, count - steps))
    return lax.ppermute(value, axis, [(source, source + steps) for source in range(first, last)])


def causal_taps(series, kernel):
    taps = kernel.shape[0]
    length = series.shape[0] - (taps - 1)
    summed = kernel[0] * series[taps - 1 : taps - 1 + length]
    for offset in range(1, taps):
        summed = summed + kernel[offset] * series[taps - 1 - offset : taps - 1 - offset + length]
    return summed


def anti_taps(series, kernel):
    taps = kernel.shape[0]
    length = series.shape[0] - (taps - 1)
    summed = kernel[0] * series[0:length]
    for offset in range(1, taps):
        summed = summed + kernel[offset] * series[offset : offset + length]
    return summed


def featurize(window, feat_taps, inner_taps):
    query_feat = causal_taps(window[6:, 0], feat_taps[0])
    key_feat = causal_taps(window[:, 1], feat_taps[1])
    value_feat = causal_taps(window[:, 2], feat_taps[2])
    inner_conv = causal_taps(key_feat * value_feat, inner_taps)
    return (query_feat, key_feat, value_feat, inner_conv)


def adjoint_rows(series, feat_taps):
    stacked = jnp.stack(
        [
            anti_taps(series[:, 0], feat_taps[0]),
            anti_taps(series[:, 1], feat_taps[1]),
            anti_taps(series[:, 2], feat_taps[2]),
        ],
        axis=1,
    ).astype(jnp.bfloat16)
    return stacked.reshape(stacked.shape[0], 3 * stacked.shape[2])


def local(tokens, proj_weight, feat_taps, inner_taps, grad_out):
    channels = proj_weight.shape[2]
    flat_weight = proj_weight.reshape(proj_weight.shape[0], 3 * channels)
    projected = jnp.dot(
        lax.all_gather(tokens, "tp", axis=0, tiled=True),
        flat_weight,
        preferred_element_type=jnp.float32,
    ).astype(jnp.bfloat16)
    row_count = projected.shape[0]
    projected = projected.reshape(row_count, 3, channels)
    earlier = from_behind(projected[row_count - 8 :], "ctx", 1)
    window = jnp.concatenate([earlier, projected], axis=0).astype(jnp.float32)
    query_feat, key_feat, value_feat, inner_conv = featurize(window, feat_taps, inner_taps)
    gated = (query_feat * inner_conv).astype(jnp.bfloat16)
    grad_f = grad_out.astype(jnp.float32)
    grad_query = grad_f * inner_conv
    grad_inner = grad_f * query_feat
    leading_mix = anti_taps(grad_inner[:8], inner_taps)
    leading = jnp.stack(
        [grad_query[:2], leading_mix * value_feat[6:8], leading_mix * key_feat[6:8]], axis=1
    )
    received, received_inner = from_behind((leading, grad_inner[:6]), "ctx", -1)
    grad_mix = anti_taps(jnp.concatenate([grad_inner, received_inner], axis=0), inner_taps)
    grad_key = jnp.concatenate([grad_mix * value_feat[6:], received[:, 1]], axis=0)
    grad_value = jnp.concatenate([grad_mix * key_feat[6:], received[:, 2]], axis=0)
    grad_query = jnp.concatenate([grad_query, received[:, 0]], axis=0)
    grad_series = jnp.stack([grad_query, grad_key, grad_value], axis=1)
    grad_proj = adjoint_rows(grad_series, feat_taps)
    grad_tokens = lax.psum_scatter(
        lax.dot_general(
            grad_proj, flat_weight, (((1,), (1,)), ((), ())), preferred_element_type=jnp.float32
        ).astype(jnp.bfloat16),
        "tp",
        scatter_dimension=0,
        tiled=True,
    )
    return (gated, grad_tokens)


def solution(mesh):
    in_specs = (
        P(("ctx", "tp"), None),
        P(None, None, "tp"),
        P(None, None, "tp"),
        P(None, "tp"),
        P("ctx", "tp"),
    )
    out_specs = (P("ctx", "tp"), P(("ctx", "tp"), None))
    return jax.shard_map(local, mesh=mesh, in_specs=in_specs, out_specs=out_specs, check_vma=False)
```

profile of v0, /device:TPU:4, one launch (start us, length us, event | category | flops | bytes accessed | tf_op | source)
XLA Modules:
  0.0 119.4 jit_solution(3419005539408594490)
XLA Ops:
  7.2 0.0 reduce-scatter.2.cloned.1.call-start
  7.2 20.1 %all_gather.3 = bf16[96,4096]{1,0:T(8,128)(2,1)S(1)} all-gather(bf16[24,4096]{1,0:T(8,128)(2,1)} %param.5), channel_id=1, replica_groups=mesh['ctx'=8,'tp'=4] {'tp'}, dimensions={0}, use_global_device_ids=true | all-gather | bytes 983040 | tf_op jit(solution)/shard_map/all_gather | solution.py:55
  27.3 23.6 %copy.8 = bf16[4096,3,768]{0,2,1:T(8,128)(2,1)} copy(bf16[4096,3,768]{2,0,1:T(8,128)(2,1)} %param.6) | data formatting | bytes 37748736 | tf_op args[1]
  50.9 0.0 copy-start.2
  50.9 0.0 copy-start.1
  50.9 0.0 copy-start
  50.9 12.3 %convolution_convert_fusion = bf16[96,2304]{1,0:T(8,128)(2,1)S(1)} fusion(bf16[96,4096]{1,0:T(8,128)(2,1)S(1)} %all_gather.3, bf16[4096,2304]{0,1:T(8,128)(2,1)} %bitcast.100), kind=kOutput, calls=%fused_computation.2 | convolution fusion | flops 1812160512 | bytes 20103168 | tf_op jit(solution)/shard_map/dot_general | solution.py:54
  63.2 1.9 %collective-permute-start = (bf16[8,3,768]{2,0,1:T(8,128)(2,1)S(1)}, bf16[8,3,768]{2,0,1:T(8,128)(2,1)S(1)}, u32[]{:S(2)}, u32[]{:S(2)}) collective-permute-start(bf16[8,3,768]{2,0,1:T(8,128)(2,1)S(1)} %bitcast.103), channel_id=1, source_target_pairs={{0,4},{4,8},{8,12},{12,16},{16,20},{20,24},{24,28},{1,5},{5,9},{9,... | collective-permute-start | bytes 110600 | tf_op jit(solution)/shard_map/ppermute | solution.py:10
  65.2 0.0 copy-done.2
  65.2 0.1 slice_reduce_fusion.12
  65.3 0.0 copy-done.1
  65.3 0.1 slice_reduce_fusion.8
  65.4 4.0 %collective-permute-done = bf16[8,3,768]{2,0,1:T(8,128)(2,1)S(1)} collective-permute-done((bf16[8,3,768]{2,0,1:T(8,128)(2,1)S(1)}, bf16[8,3,768]{2,0,1:T(8,128)(2,1)S(1)}, u32[]{:S(2)}, u32[]{:S(2)}) %collective-permute-start) | collective-permute-done | bytes 36896 | tf_op jit(solution)/shard_map/ppermute | solution.py:10
  69.4 0.1 maximum_convert_fusion
  69.5 0.0 copy-done
  69.5 0.1 convert_multiply_fusion
  69.6 0.2 fusion.78
  69.8 0.3 convert_multiply_fusion.1
  70.2 1.9 %collective-permute-start.2 = (f32[6,768]{1,0:T(8,128)S(1)}, f32[6,768]{1,0:T(8,128)S(1)}, u32[]{:S(2)}, u32[]{:S(2)}) collective-permute-start(f32[6,768]{1,0:T(8,128)S(1)} %slice.381), channel_id=1, source_target_pairs={{4,0},{8,4},{12,8},{16,12},{20,16},{24,20},{28,24},{5,1},{9,5},{13... | collective-permute-start | bytes 55304 | tf_op jit(solution)/shard_map/ppermute | solution.py:10
  72.1 2.5 %collective-permute-start.1 = (f32[2,3,768]{2,0,1:T(2,128)S(1)}, f32[2,3,768]{2,0,1:T(2,128)S(1)}, u32[]{:S(2)}, u32[]{:S(2)}) collective-permute-start(f32[2,3,768]{2,0,1:T(2,128)S(1)} %pad_maximum_fusion.4), channel_id=1, source_target_pairs={{4,0},{8,4},{12,8},{16,12},{20,16},{24,20},{28,24},{5,1},{9,5},{13... | collective-permute-start | bytes 55304 | tf_op jit(solution)/shard_map/ppermute | solution.py:10
  74.7 0.0 collective-permute-done.2
  74.7 0.3 slice_multiply_fusion.1
  75.0 1.1 collective-permute-done.1
  76.1 0.1 fusion.64
  76.2 0.2 fusion.62
  76.4 13.0 %fusion = bf16[96,4096]{1,0:T(8,128)(2,1)} fusion(bf16[4096,3,768]{2,0,1:T(8,128)(2,1)} %param.6, bf16[96,1,768]{2,0,1:T(8,128)(2,1)S(1)} %fusion.64, bf16[96,1,768]{2,0,1:T(8,128)(2,1)S(1)} %get-tuple-element.33, bf16[96,1,768]{2,0,1:T(8,128)(2,1)S(1)} %get-tuple-element.32), kind=kOutput, calls=%fused_computation.1 | convolution fusion | flops 1812774912 | bytes 20103168 | tf_op jit(solution)/shard_map/dot_general | solution.py:80
  89.5 0.0 reduce-scatter.2.cloned.1.call-update
  89.5 0.7 multiply_convert_fusion
  90.2 22.4 %reduce-scatter.2.cloned.1.call-done = bf16[24,4096]{1,0:T(8,128)(2,1)} async-done(((bf16[96,4096]{1,0:T(8,128)(2,1)}), bf16[24,4096]{1,0:T(8,128)(2,1)}) %reduce-scatter.2.cloned.1.call-update) | async-done | bytes 196624 | tf_op jit(solution)/shard_map/reduce_scatter | solution.py:79
  (9 shorter events, 0.1 us)
Async XLA Ops:
  7.2 105.4 %reduce-scatter.2.cloned.1.call-start = ((), (), s32[]{:S(2)}) async-start(), calls=%async_computation.1 | async-start | bytes 983040 | tf_op jit(solution)/shard_map/reduce_scatter | solution.py:79
  50.9 14.3 %copy-start.2 = (f32[7,768]{1,0:T(8,128)S(1)}, f32[7,768]{1,0:T(8,128)}, u32[]{:S(2)}) copy-start(f32[7,768]{1,0:T(8,128)} %param.8) | copy-start | bytes 64516
  50.9 14.3 %copy-start.1 = (f32[3,3,768]{2,1,0:T(4,128)S(1)}, f32[3,3,768]{2,1,0:T(4,128)}, u32[]{:S(2)}) copy-start(f32[3,3,768]{2,1,0:T(4,128)} %param.7) | copy-start | bytes 82948
  50.9 18.6 %copy-start = (bf16[96,768]{1,0:T(8,128)(2,1)S(1)}, bf16[96,768]{1,0:T(8,128)(2,1)}, u32[]{:S(2)}) copy-start(bf16[96,768]{1,0:T(8,128)(2,1)} %param.9) | copy-start | bytes 442372
  63.2 6.2 %collective-permute-start = (bf16[8,3,768]{2,0,1:T(8,128)(2,1)S(1)}, bf16[8,3,768]{2,0,1:T(8,128)(2,1)S(1)}, u32[]{:S(2)}, u32[]{:S(2)}) collective-permute-start(bf16[8,3,768]{2,0,1:T(8,128)(2,1)S(1)} %bitcast.103), channel_id=1, source_target_pairs={{0,4},{4,8},{8,12},{12,16},{16,20},{20,24},{24,28},{1,5},{5,9},{9,... | collective-permute-start | bytes 110600 | tf_op jit(solution)/shard_map/ppermute | solution.py:10
  70.2 4.5 %collective-permute-start.2 = (f32[6,768]{1,0:T(8,128)S(1)}, f32[6,768]{1,0:T(8,128)S(1)}, u32[]{:S(2)}, u32[]{:S(2)}) collective-permute-start(f32[6,768]{1,0:T(8,128)S(1)} %slice.381), channel_id=1, source_target_pairs={{4,0},{8,4},{12,8},{16,12},{20,16},{24,20},{28,24},{5,1},{9,5},{13... | collective-permute-start | bytes 55304 | tf_op jit(solution)/shard_map/ppermute | solution.py:10
  72.1 4.0 %collective-permute-start.1 = (f32[2,3,768]{2,0,1:T(2,128)S(1)}, f32[2,3,768]{2,0,1:T(2,128)S(1)}, u32[]{:S(2)}, u32[]{:S(2)}) collective-permute-start(f32[2,3,768]{2,0,1:T(2,128)S(1)} %pad_maximum_fusion.4), channel_id=1, source_target_pairs={{4,0},{8,4},{12,8},{16,12},{20,16},{24,20},{28,24},{5,1},{9,5},{13... | collective-permute-start | bytes 55304 | tf_op jit(solution)/shard_map/ppermute | solution.py:10
Sparse Core Ops, SparseCore 0:
  89.6 22.8 reduce-scatter.1
where the time goes:
time: 122 us; the launch traced here: 119 us
  waiting for transfers between devices  27.5 us (23%)
  matrix products  25.3 us (21%)
  local copies, waits for them, and re-layouts  23.8 us (20%)
  blocking collectives  20.1 us (16%)
  between operations  14.2 us (12%)
  starting transfers between devices  6.42 us (5%)
  other arithmetic  2.04 us (2%)
    unnamed x7, local copies, waits for them, and re-layouts  23.7 us
    reduce_scatter x1, waiting for transfers between devices, local(): lax.psum_scatter(lax.dot_general(grad_proj, flat_weight, (((1,), (1,)), (...  22.4 us
    all_gather x1, blocking collectives, local(): lax.all_gather(tokens, 'tp', axis=0, tiled=True)  20.1 us
    dot_general x1, matrix products, local(): lax.dot_general(grad_proj, flat_weight, (((1,), (1,)), ((), ())), preferr...  13 us
    dot_general x1, matrix products, local(): jnp.dot(lax.all_gather(tokens, 'tp', axis=0, tiled=True), flat_weight, pr...  12.3 us
    ppermute x3, starting transfers between devices, from_behind(): lax.ppermute(value, axis, [(source, source + steps) for source in range(f...  6.39 us
    ppermute x3, waiting for transfers between devices, from_behind(): lax.ppermute(value, axis, [(source, source + steps) for source in range(f...  5.13 us
  transfers between devices with their start and end apart: 4, of which 3 were waited for; matrix products, arithmetic and copies ran while one was open for 1% of the time, Pallas kernels for 0%

commit v1 on v0

v1 whole, which is shorter than its diff:
```python
import functools

import jax
import jax.numpy as jnp
from jax import lax
from jax.experimental import pallas as pl
from jax.experimental.pallas import tpu as pltpu
from jax.sharding import PartitionSpec as P

MESH = pl.DeviceIdType.MESH
F32 = jnp.float32
BF16 = jnp.bfloat16
PIECES = 4
HALO = 8


def kernel(
    n,
    n_ctx,
    tokens,
    weight_hbm,
    feat_taps,
    inner_taps,
    grad_out,
    gated,
    grad_tokens,
    weight,
    blocks,
    stack,
    ext,
    grads,
    mix,
    dinner,
    dfeat,
    dproj,
    edge,
    halo,
    grad_edge,
    grad_halo,
    partial,
    outgoing,
    from_left,
    from_right,
    weight_sem,
    gather_recv,
    gather_right,
    gather_left,
    scatter_send,
    left_recv,
    right_recv,
    halo_send,
    halo_recv,
):
    z = lax.axis_index("tp")
    ctx = lax.axis_index("ctx")
    rows, width = tokens.shape
    total, channels = gated.shape
    cut = width // PIECES

    def weight_copy(piece, part):
        span = pl.ds(piece * cut, cut)
        return pltpu.make_async_copy(
            weight_hbm.at[part, span, :], weight.at[part, span, :], weight_sem.at[piece, part]
        )

    for piece in range(PIECES):
        for part in range(3):
            weight_copy(piece, part).start()

    has_left, has_right = z > 0, z < n - 1
    has_before, has_after = ctx > 0, ctx < n_ctx - 1
    barrier = pltpu.get_barrier_semaphore()

    def greet(here, axis, index):
        @pl.when(here)
        def _():
            pl.semaphore_signal(barrier, inc=1, device_id={axis: index}, device_id_type=MESH)

    greet(has_left, "tp", z - 1)
    greet(has_right, "tp", z + 1)
    greet(has_before, "ctx", ctx - 1)
    greet(has_after, "ctx", ctx + 1)

    for piece in range(PIECES):
        blocks[piece, z] = tokens[:, piece * cut : (piece + 1) * cut]
    grads[0:total, :] = grad_out[...].astype(F32)
    grad_edge[...] = grads[0:HALO, :]

    peers = sum(
        here.astype(jnp.int32) for here in (has_left, has_right, has_before, has_after)
    )
    pl.semaphore_wait(barrier, peers)

    def to_right(piece, block):
        return pltpu.make_async_remote_copy(
            src_ref=blocks.at[piece, block],
            dst_ref=blocks.at[piece, block],
            send_sem=gather_right.at[piece, block],
            recv_sem=gather_recv.at[piece, block],
            device_id={"tp": z + 1},
            device_id_type=MESH,
        )

    def to_left(piece, block):
        return pltpu.make_async_remote_copy(
            src_ref=blocks.at[piece, block],
            dst_ref=blocks.at[piece, block],
            send_sem=gather_left.at[piece, block],
            recv_sem=gather_recv.at[piece, block],
            device_id={"tp": z - 1},
            device_id_type=MESH,
        )

    for piece in range(PIECES):

        @pl.when(has_right)
        def _():
            to_right(piece, z).start()

        @pl.when(has_left)
        def _():
            to_left(piece, z).start()

    grad_copy = pltpu.make_async_remote_copy(
        src_ref=grad_edge,
        dst_ref=grad_halo,
        send_sem=halo_send.at[0],
        recv_sem=halo_recv.at[0],
        device_id={"ctx": ctx - 1},
        device_id_type=MESH,
    )

    @pl.when(has_before)
    def _():
        grad_copy.start()

    def gather_step(step, carry):
        for piece in range(PIECES):

            @pl.when(z - step >= 0)
            def _():
                to_right(piece, z - step).wait_recv()

                @pl.when(has_right)
                def _():
                    to_right(piece, z - step).start()

            @pl.when(z + step <= n - 1)
            def _():
                to_left(piece, z + step).wait_recv()

                @pl.when(has_left)
                def _():
                    to_left(piece, z + step).start()

        return carry

    lax.fori_loop(1, n - 1, gather_step, 0)

    for piece in range(PIECES):

        @pl.when(z == n - 1)
        def _():
            to_right(piece, 0).wait_recv()

        @pl.when(z == 0)
        def _():
            to_left(piece, n - 1).wait_recv()

        for block in range(n):
            stack[block * rows : (block + 1) * rows, :] = blocks[piece, block].astype(F32)
        left_side = stack[...].astype(BF16)
        for part in range(3):
            weight_copy(piece, part).wait()
            product = jnp.dot(
                left_side,
                weight[part, piece * cut : (piece + 1) * cut, :],
                preferred_element_type=F32,
            )
            if piece == 0:
                ext[part, HALO : HALO + total, :] = product
            else:
                ext[part, HALO : HALO + total, :] += product

    edge[0] = ext[:, HALO : 2 * HALO, :]
    edge[1] = ext[:, total : total + HALO, :]

    def edge_copy(side, target):
        return pltpu.make_async_remote_copy(
            src_ref=edge.at[side],
            dst_ref=halo.at[side],
            send_sem=halo_send.at[1 + side],
            recv_sem=halo_recv.at[1 + side],
            device_id={"ctx": target},
            device_id_type=MESH,
        )

    first_rows = edge_copy(0, ctx - 1)
    last_rows = edge_copy(1, ctx + 1)

    @pl.when(has_before)
    def _():
        first_rows.start()

    @pl.when(has_after)
    def _():
        last_rows.start()

    @pl.when(has_after)
    def _():
        grad_copy.wait_recv()
        grads[total : total + HALO, :] = grad_halo[...]
        first_rows.wait_recv()
        ext[:, HALO + total :, :] = halo[0]

    @pl.when(ctx == n_ctx - 1)
    def _():
        grads[total : total + HALO, :] = jnp.zeros((HALO, channels), F32)
        ext[:, HALO + total :, :] = jnp.zeros((3, HALO, channels), F32)

    @pl.when(has_before)
    def _():
        last_rows.wait_recv()
        ext[:, 0:HALO, :] = halo[1]

    @pl.when(ctx == 0)
    def _():
        ext[:, 0:HALO, :] = jnp.zeros((3, HALO, channels), F32)

    long = total + HALO
    lanes = 128

    def channel_step(index, carry):
        at = pl.ds(pl.multiple_of(index * lanes, lanes), lanes)

        def conv(part, start):
            terms = feat_taps[part, 0:1, at] * ext[part, start : start + long, at]
            for tap in range(1, 3):
                terms += (
                    feat_taps[part, tap : tap + 1, at]
                    * ext[part, start - tap : start - tap + long, at]
                )
            return terms

        query = conv(0, HALO)
        dinner[0:long, :] = grads[:, at] * query
        key = conv(1, 2)
        value = conv(2, 2)
        mix[0:long, :] = key * value
        dfeat[1, 0:long, :] = value
        dfeat[2, 0:long, :] = key
        inner = inner_taps[0:1, at] * mix[6 : 6 + long, :]
        for tap in range(1, 7):
            inner += inner_taps[tap : tap + 1, at] * mix[6 - tap : 6 - tap + long, :]
        gated[:, at] = (query * inner)[0:total].astype(BF16)
        dfeat[0, 0:long, :] = grads[:, at] * inner
        dmix = inner_taps[0:1, at] * dinner[0:long, :]
        for tap in range(1, 7):
            dmix += inner_taps[tap : tap + 1, at] * dinner[tap : tap + long, :]
        dkey = dmix * dfeat[1, 6 : 6 + long, :]
        dvalue = dmix * dfeat[2, 6 : 6 + long, :]
        dfeat[1, 0:long, :] = dkey
        dfeat[2, 0:long, :] = dvalue
        for part in range(3):
            series = feat_taps[part, 0:1, at] * dfeat[part, 0:total, :]
            for tap in range(1, 3):
                series += feat_taps[part, tap : tap + 1, at] * dfeat[part, tap : tap + total, :]
            dproj[part, :, at] = series.astype(BF16)
        return carry

    tail = jnp.zeros((HALO, lanes), F32)
    mix[long:, :] = tail
    dinner[long:, :] = tail
    for part in range(3):
        dfeat[part, long:, :] = tail
    lax.fori_loop(0, channels // lanes, channel_step, 0)

    def pass_right(piece, block):
        return pltpu.make_async_remote_copy(
            src_ref=outgoing.at[piece, block],
            dst_ref=from_left.at[piece, block],
            send_sem=scatter_send.at[piece, block],
            recv_sem=left_recv.at[piece, block],
            device_id={"tp": z + 1},
            device_id_type=MESH,
        )

    def pass_left(piece, block):
        return pltpu.make_async_remote_copy(
            src_ref=outgoing.at[piece, block],
            dst_ref=from_right.at[piece, block],
            send_sem=scatter_send.at[piece, block],
            recv_sem=right_recv.at[piece, block],
            device_id={"tp": z - 1},
            device_id_type=MESH,
        )

    def begin(piece):
        def step_of(step, carry):
            far, near = n - 1 - step, step

            @pl.when(z == 0)
            def _():
                outgoing[piece, far] = partial[piece, far].astype(BF16)
                pass_right(piece, far).start()

            @pl.when(z == n - 1)
            def _():
                outgoing[piece, near] = partial[piece, near].astype(BF16)
                pass_left(piece, near).start()

            return carry

        lax.fori_loop(0, n - 1, step_of, 0)

    def forward(piece):
        def step_of(step, carry):
            far, near = n - 1 - step, step

            @pl.when((z > 0) & (z < far))
            def _():
                pass_right(piece, far).wait_recv()
                outgoing[piece, far] = (
                    from_left[piece, far].astype(F32) + partial[piece, far]
                ).astype(BF16)
                pass_right(piece, far).start()

            @pl.when((z < n - 1) & (z > near))
            def _():
                pass_left(piece, near).wait_recv()
                outgoing[piece, near] = (
                    from_right[piece, near].astype(F32) + partial[piece, near]
                ).astype(BF16)
                pass_left(piece, near).start()

            return carry

        lax.fori_loop(0, n - 1, step_of, 0)

    for piece in range(PIECES):
        share = jnp.zeros((total, cut), F32)
        for part in range(3):
            share += lax.dot_general(
                dproj[part],
                weight[part, piece * cut : (piece + 1) * cut, :],
                (((1,), (1,)), ((), ())),
                preferred_element_type=F32,
            )
        for block in range(n):
            partial[piece, block] = share[block * rows : (block + 1) * rows]
        begin(piece)
        if piece > 0:
            forward(piece - 1)
    forward(PIECES - 1)

    for piece in range(PIECES):

        @pl.when(has_left)
        def _():
            pass_right(piece, z).wait_recv()
            partial[piece, z] += from_left[piece, z].astype(F32)

        @pl.when(has_right)
        def _():
            pass_left(piece, z).wait_recv()
            partial[piece, z] += from_right[piece, z].astype(F32)

        grad_tokens[:, piece * cut : (piece + 1) * cut] = partial[piece, z].astype(BF16)

    @pl.when(has_before)
    def _():
        grad_copy.wait_send()
        first_rows.wait_send()

    @pl.when(has_after)
    def _():
        last_rows.wait_send()

    def drain(block, carry):
        for piece in range(PIECES):

            @pl.when(has_right & (block <= z))
            def _():
                to_right(piece, block).wait_send()

            @pl.when(has_left & (block >= z))
            def _():
                to_left(piece, block).wait_send()

            @pl.when(block != z)
            def _():
                pass_right(piece, block).wait_send()

        return carry

    lax.fori_loop(0, n, drain, 0)


def local(n, n_ctx, tokens, proj_weight, feat_taps, inner_taps, grad_out):
    rows, width = tokens.shape
    total, channels = grad_out.shape
    cut = width // PIECES
    weight = jnp.transpose(proj_weight, (1, 0, 2))
    vmem = pl.BlockSpec(memory_space=pltpu.VMEM)
    dma = pltpu.SemaphoreType.DMA
    long = total + 2 * HALO
    return pl.pallas_call(
        functools.partial(kernel, n, n_ctx),
        out_shape=(
            jax.ShapeDtypeStruct((total, channels), BF16),
            jax.ShapeDtypeStruct((rows, width), BF16),
        ),
        in_specs=[vmem, pl.BlockSpec(memory_space=pl.ANY), vmem, vmem, vmem],
        out_specs=(vmem, vmem),
        scratch_shapes=[
            pltpu.VMEM((3, width, channels), BF16),
            pltpu.VMEM((PIECES, n, rows, cut), BF16),
            pltpu.VMEM((total, cut), F32),
            pltpu.VMEM((3, long, channels), F32),
            pltpu.VMEM((total + HALO, channels), F32),
            pltpu.VMEM((long, 128), F32),
            pltpu.VMEM((long, 128), F32),
            pltpu.VMEM((3, long, 128), F32),
            pltpu.VMEM((3, total, channels), BF16),
            pltpu.VMEM((2, 3, HALO, channels), F32),
            pltpu.VMEM((2, 3, HALO, channels), F32),
            pltpu.VMEM((HALO, channels), F32),
            pltpu.VMEM((HALO, channels), F32),
            pltpu.VMEM((PIECES, n, rows, cut), F32),
            pltpu.VMEM((PIECES, n, rows, cut), BF16),
            pltpu.VMEM((PIECES, n, rows, cut), BF16),
            pltpu.VMEM((PIECES, n, rows, cut), BF16),
            dma((PIECES, 3)),
            dma((PIECES, n)),
            dma((PIECES, n)),
            dma((PIECES, n)),
            dma((PIECES, n)),
            dma((PIECES, n)),
            dma((PIECES, n)),
            dma((3,)),
            dma((3,)),
        ],
        compiler_params=pltpu.CompilerParams(
            collective_id=0, has_side_effects=True, vmem_limit_bytes=50 * 1024 * 1024
        ),
        cost_estimate=pl.CostEstimate(
            flops=4 * total * width * 3 * channels,
            bytes_accessed=6 * width * channels,
            transcendentals=0,
        ),
    )(tokens, weight, feat_taps, inner_taps, grad_out)


def solution(mesh):
    in_specs = (
        P(("ctx", "tp"), None),
        P(None, None, "tp"),
        P(None, None, "tp"),
        P(None, "tp"),
        P("ctx", "tp"),
    )
    out_specs = (P("ctx", "tp"), P(("ctx", "tp"), None))
    body = functools.partial(local, mesh.shape["tp"], mesh.shape["ctx"])
    return jax.shard_map(
        body, mesh=mesh, in_specs=in_specs, out_specs=out_specs, check_vma=False
    )
```

time: 122 us -> 68.8 us (0.56); the launches traced: 119 us -> 68.5 us
  Pallas kernels: 0 us -> 63.2 us
  waiting for transfers between devices: 27.5 us -> 0 us
  matrix products: 25.3 us -> 0 us
  blocking collectives: 20.1 us -> 0 us
  local copies, waits for them, and re-layouts: 23.8 us -> 4.67 us
  between operations: 14.2 us -> 0.65 us
  starting transfers between devices: 6.42 us -> 0 us
  other arithmetic: 2.04 us -> 0 us
    pallas_call x0 -> x1, Pallas kernels: none -> 63.2 us  [local(): pl.pallas_call(functools.partial(kernel, n, n_ctx), out_shape=(jax.ShapeD...]
    dot_general x2 -> x0, matrix products: 25.3 us -> none  [the longest x1 13 us: local(): lax.dot_general(grad_proj, flat_weight, (((1,), (1,)), ((), ())), preferr...]
    reduce_scatter x1 -> x0, waiting for transfers between devices: 22.4 us -> none  [local(): lax.psum_scatter(lax.dot_general(grad_proj, flat_weight, (((1,), (1,)), (...]
    all_gather x1 -> x0, blocking collectives: 20.1 us -> none  [local(): lax.all_gather(tokens, 'tp', axis=0, tiled=True)]
    unnamed x7 -> x10, local copies, waits for them, and re-layouts: 23.7 us -> 4.67 us
    ppermute x3 -> x0, starting transfers between devices: 6.39 us -> none  [from_behind(): lax.ppermute(value, axis, [(source, source + steps) for source in range(f...]
    ppermute x3 -> x0, waiting for transfers between devices: 5.13 us -> none  [from_behind(): lax.ppermute(value, axis, [(source, source + steps) for source in range(f...]
  transfers between devices with their start and end apart: 4 -> 0, of which waited for: 3 -> 0; matrix products, arithmetic and copies ran while one was open for 1% -> 0% of each run, Pallas kernels for 0% -> 0%
where the time goes in v1:
time: 68.8 us; the launch traced here: 68.5 us
  Pallas kernels  63.2 us (92%)
  local copies, waits for them, and re-layouts  4.67 us (7%)
    pallas_call x1, Pallas kernels, local(): pl.pallas_call(functools.partial(kernel, n, n_ctx), out_shape=(jax.ShapeD...  63.2 us
    unnamed x10, local copies, waits for them, and re-layouts  4.67 us

profile of v1, /device:TPU:4, one launch (start us, length us, event | category | flops | bytes accessed | tf_op | source)
XLA Modules:
  0.0 68.5 jit_solution(13205807452160050872)
XLA Ops:
  0.6 0.0 copy-start
  0.6 0.9 %copy-done = bf16[24,4096]{1,0:T(8,128)(2,1)S(1)} copy-done((bf16[24,4096]{1,0:T(8,128)(2,1)S(1)}, bf16[24,4096]{1,0:T(8,128)(2,1)}, u32[]{:S(2)}) %copy-start) | copy-done | bytes 196632
  1.6 0.0 copy-start.1
  1.6 0.9 %copy-done.1 = bf16[96,768]{1,0:T(8,128)(2,1)S(1)} copy-done((bf16[96,768]{1,0:T(8,128)(2,1)S(1)}, bf16[96,768]{1,0:T(8,128)(2,1)}, u32[]{:S(2)}) %copy-start.1) | copy-done | bytes 147480
  2.5 0.0 copy-start.2
  2.5 0.8 %copy-done.2 = f32[3,3,768]{2,1,0:T(4,128)S(1)} copy-done((f32[3,3,768]{2,1,0:T(4,128)S(1)}, f32[3,3,768]{2,1,0:T(4,128)}, u32[]{:S(2)}) %copy-start.2) | copy-done | bytes 27672
  3.2 0.0 copy-start.3
  3.2 0.7 %copy-done.3 = f32[7,768]{1,0:T(8,128)S(1)} copy-done((f32[7,768]{1,0:T(8,128)S(1)}, f32[7,768]{1,0:T(8,128)}, u32[]{:S(2)}) %copy-start.3) | copy-done | bytes 21528
  4.0 63.2 %shard_map.68 = (bf16[96,768]{1,0:T(8,128)(2,1)S(1)}, bf16[24,4096]{1,0:T(8,128)(2,1)S(1)}) custom-call(bf16[24,4096]{1,0:T(8,128)(2,1)S(1)} %copy-done, bf16[3,4096,768]{2,1,0:T(8,128)(2,1)} %bitcast.1, f32[3,3,768]{2,1,0:T(4,128)S(1)} %copy-done.2, f32[7,768]{1,0:T(8,128)S(1)} %copy-done.3, bf16[96,768]{1,0:T(8,128)(2,1)S(1)} %copy-done.1), custom_call_target="tpu_custom_call" | custom-call | flops 3623878656 | bytes 18874368 | tf_op jit(solution)/shard_map/pallas_call | solution.py:407
  67.1 0.7 copy.9
  67.8 0.7 copy.10
Async XLA Ops:
  0.6 0.9 %copy-start = (bf16[24,4096]{1,0:T(8,128)(2,1)S(1)}, bf16[24,4096]{1,0:T(8,128)(2,1)}, u32[]{:S(2)}) copy-start(bf16[24,4096]{1,0:T(8,128)(2,1)} %tokens.1) | copy-start | bytes 589828
  1.6 0.9 %copy-start.1 = (bf16[96,768]{1,0:T(8,128)(2,1)S(1)}, bf16[96,768]{1,0:T(8,128)(2,1)}, u32[]{:S(2)}) copy-start(bf16[96,768]{1,0:T(8,128)(2,1)} %grad_out.1) | copy-start | bytes 442372
  2.5 0.8 %copy-start.2 = (f32[3,3,768]{2,1,0:T(4,128)S(1)}, f32[3,3,768]{2,1,0:T(4,128)}, u32[]{:S(2)}) copy-start(f32[3,3,768]{2,1,0:T(4,128)} %feat_taps.1) | copy-start | bytes 82948
  3.2 0.7 %copy-start.3 = (f32[7,768]{1,0:T(8,128)S(1)}, f32[7,768]{1,0:T(8,128)}, u32[]{:S(2)}) copy-start(f32[7,768]{1,0:T(8,128)} %inner_taps.1) | copy-start | bytes 64516

commit v2 on v1

--- a/solution.py
+++ b/solution.py
@@ -19,11 +19,14 @@
     n_ctx,
     tokens,
     weight_hbm,
+    feat_hbm,
+    inner_hbm,
+    grad_hbm,
+    gated,
+    grad_tokens,
     feat_taps,
     inner_taps,
     grad_out,
-    gated,
-    grad_tokens,
     weight,
     blocks,
     stack,
@@ -50,6 +53,8 @@
     right_recv,
     halo_send,
     halo_recv,
+    token_sem,
+    small_sem,
 ):
     z = lax.axis_index("tp")
     ctx = lax.axis_index("ctx")
@@ -63,6 +68,20 @@
             weight_hbm.at[part, span, :], weight.at[part, span, :], weight_sem.at[piece, part]
         )
 
+    own = [
+        pltpu.make_async_copy(
+            tokens.at[:, pl.ds(piece * cut, cut)], blocks.at[piece, z], token_sem.at[piece]
+        )
+        for piece in range(PIECES)
+    ]
+    small = [
+        pltpu.make_async_copy(source, target, small_sem.at[index])
+        for index, (source, target) in enumerate(
+            ((grad_hbm, grad_out), (feat_hbm, feat_taps), (inner_hbm, inner_taps))
+        )
+    ]
+    for copy in own + small:
+        copy.start()
     for piece in range(PIECES):
         for part in range(3):
             weight_copy(piece, part).start()
@@ -81,8 +100,8 @@
     greet(has_before, "ctx", ctx - 1)
     greet(has_after, "ctx", ctx + 1)
 
-    for piece in range(PIECES):
-        blocks[piece, z] = tokens[:, piece * cut : (piece + 1) * cut]
+    for copy in own + small:
+        copy.wait()
     grads[0:total, :] = grad_out[...].astype(F32)
     grad_edge[...] = grads[0:HALO, :]
 
@@ -338,14 +357,15 @@
         lax.fori_loop(0, n - 1, step_of, 0)
 
     for piece in range(PIECES):
-        share = jnp.zeros((total, cut), F32)
+        turned = jnp.zeros((cut, total), F32)
         for part in range(3):
-            share += lax.dot_general(
+            turned += lax.dot_general(
+                weight[part, piece * cut : (piece + 1) * cut, :],
                 dproj[part],
-                weight[part, piece * cut : (piece + 1) * cut, :],
                 (((1,), (1,)), ((), ())),
                 preferred_element_type=F32,
             )
+        share = turned.T
         for block in range(n):
             partial[piece, block] = share[block * rows : (block + 1) * rows]
         begin(piece)
@@ -410,9 +430,12 @@
             jax.ShapeDtypeStruct((total, channels), BF16),
             jax.ShapeDtypeStruct((rows, width), BF16),
         ),
-        in_specs=[vmem, pl.BlockSpec(memory_space=pl.ANY), vmem, vmem, vmem],
+        in_specs=[pl.BlockSpec(memory_space=pl.ANY)] * 5,
         out_specs=(vmem, vmem),
         scratch_shapes=[
+            pltpu.VMEM(feat_taps.shape, F32),
+            pltpu.VMEM(inner_taps.shape, F32),
+            pltpu.VMEM((total, channels), BF16),
             pltpu.VMEM((3, width, channels), BF16),
             pltpu.VMEM((PIECES, n, rows, cut), BF16),
             pltpu.VMEM((total, cut), F32),
@@ -439,9 +462,11 @@
             dma((PIECES, n)),
             dma((3,)),
             dma((3,)),
+            dma((PIECES,)),
+            dma((3,)),
         ],
         compiler_params=pltpu.CompilerParams(
-            collective_id=0, has_side_effects=True, vmem_limit_bytes=50 * 1024 * 1024
+            collective_id=0, has_side_effects=True, vmem_limit_bytes=58 * 1024 * 1024
         ),
         cost_estimate=pl.CostEstimate(
             flops=4 * total * width * 3 * channels,

time: 68.8 us -> 71.7 us (1.042)
  Pallas kernels: 63.2 us -> 67.7 us
  local copies, waits for them, and re-layouts: 4.67 us -> 3.2 us
    pallas_call x1, Pallas kernels: 63.2 us -> 67.7 us  [local(): pl.pallas_call(functools.partial(kernel, n, n_ctx), out_shape=(jax.ShapeD...]
    unnamed x10 -> x2, local copies, waits for them, and re-layouts: 4.67 us -> 3.2 us
where the time goes in v2:
time: 71.7 us; the launch traced here: 71.6 us
  Pallas kernels  67.7 us (94%)
  local copies, waits for them, and re-layouts  3.2 us (4%)
    pallas_call x1, Pallas kernels, local(): pl.pallas_call(functools.partial(kernel, n, n_ctx), out_shape=(jax.ShapeD...  67.7 us
    unnamed x2, local copies, waits for them, and re-layouts  3.2 us

profile of v2, /device:TPU:4, one launch (start us, length us, event | category | flops | bytes accessed | tf_op | source)
XLA Modules:
  0.0 71.6 jit_solution(9023147306776469640)
XLA Ops:
  0.6 67.7 %shard_map.68 = (bf16[96,768]{1,0:T(8,128)(2,1)}, bf16[24,4096]{1,0:T(8,128)(2,1)}) custom-call(bf16[24,4096]{1,0:T(8,128)(2,1)} %tokens.1, bf16[3,4096,768]{2,1,0:T(8,128)(2,1)} %bitcast.1, f32[3,3,768]{2,1,0:T(4,128)} %feat_hbm.1, f32[7,768]{1,0:T(8,128)} %inner_hbm.1, bf16[96,768]{1,0:T(8,128)(2,1)} %grad_hbm.1), custom_call_target="tpu_custom_call" | custom-call | flops 3623878656 | bytes 18874368 | tf_op jit(solution)/shard_map/pallas_call | solution.py:427
  68.4 1.6 %copy.9 = bf16[96,768]{1,0:T(8,128)(2,1)} copy(bf16[96,768]{1,0:T(8,128)(2,1)} %get-tuple-element.4) | data formatting | bytes 294912
  70.0 1.6 %copy.10 = bf16[24,4096]{1,0:T(8,128)(2,1)} copy(bf16[24,4096]{1,0:T(8,128)(2,1)} %get-tuple-element.5) | data formatting | bytes 393216

commit v3 on v2

--- a/solution.py
+++ b/solution.py
@@ -10,7 +10,7 @@
 MESH = pl.DeviceIdType.MESH
 F32 = jnp.float32
 BF16 = jnp.bfloat16
-PIECES = 4
+PIECES = 8
 HALO = 8
 
 
@@ -40,17 +40,13 @@
     halo,
     grad_edge,
     grad_halo,
-    partial,
     outgoing,
-    from_left,
-    from_right,
+    incoming,
     weight_sem,
     gather_recv,
-    gather_right,
-    gather_left,
+    gather_send,
+    scatter_recv,
     scatter_send,
-    left_recv,
-    right_recv,
     halo_send,
     halo_recv,
     token_sem,
@@ -86,17 +82,34 @@
         for part in range(3):
             weight_copy(piece, part).start()
 
-    has_left, has_right = z > 0, z < n - 1
     has_before, has_after = ctx > 0, ctx < n_ctx - 1
     barrier = pltpu.get_barrier_semaphore()
+
+    def each_peer(act):
+        def visit(index, carry):
+            far = n - 1 - index
+
+            @pl.when(z + far < n)
+            def _():
+                act(z + far)
+
+            @pl.when(z >= far)
+            def _():
+                act(z - far)
+
+            return carry
+
+        lax.fori_loop(0, n - 1, visit, 0)
 
     def greet(here, axis, index):
         @pl.when(here)
         def _():
             pl.semaphore_signal(barrier, inc=1, device_id={axis: index}, device_id_type=MESH)
 
-    greet(has_left, "tp", z - 1)
-    greet(has_right, "tp", z + 1)
+    def greet_peer(peer):
+        pl.semaphore_signal(barrier, inc=1, device_id={"tp": peer}, device_id_type=MESH)
+
+    each_peer(greet_peer)
     greet(has_before, "ctx", ctx - 1)
     greet(has_after, "ctx", ctx + 1)
 
@@ -105,40 +118,21 @@
     grads[0:total, :] = grad_out[...].astype(F32)
     grad_edge[...] = grads[0:HALO, :]
 
-    peers = sum(
-        here.astype(jnp.int32) for here in (has_left, has_right, has_before, has_after)
-    )
+    peers = n - 1 + has_before.astype(jnp.int32) + has_after.astype(jnp.int32)
     pl.semaphore_wait(barrier, peers)
 
-    def to_right(piece, block):
+    def gather_to(piece, block, peer):
         return pltpu.make_async_remote_copy(
             src_ref=blocks.at[piece, block],
             dst_ref=blocks.at[piece, block],
-            send_sem=gather_right.at[piece, block],
+            send_sem=gather_send.at[piece, peer],
             recv_sem=gather_recv.at[piece, block],
-            device_id={"tp": z + 1},
+            device_id={"tp": peer},
             device_id_type=MESH,
         )
 
-    def to_left(piece, block):
-        return pltpu.make_async_remote_copy(
-            src_ref=blocks.at[piece, block],
-            dst_ref=blocks.at[piece, block],
-            send_sem=gather_left.at[piece, block],
-            recv_sem=gather_recv.at[piece, block],
-            device_id={"tp": z - 1},
-            device_id_type=MESH,
-        )
-
-    for piece in range(PIECES):
-
-        @pl.when(has_right)
-        def _():
-            to_right(piece, z).start()
-
-        @pl.when(has_left)
-        def _():
-            to_left(piece, z).start()
+    for piece in range(PIECES):
+        each_peer(lambda peer: gather_to(piece, z, peer).start())
 
     grad_copy = pltpu.make_async_remote_copy(
         src_ref=grad_edge,
@@ -153,39 +147,8 @@
     def _():
         grad_copy.start()
 
-    def gather_step(step, carry):
-        for piece in range(PIECES):
-
-            @pl.when(z - step >= 0)
-            def _():
-                to_right(piece, z - step).wait_recv()
-
-                @pl.when(has_right)
-                def _():
-                    to_right(piece, z - step).start()
-
-            @pl.when(z + step <= n - 1)
-            def _():
-                to_left(piece, z + step).wait_recv()
-
-                @pl.when(has_left)
-                def _():
-                    to_left(piece, z + step).start()
-
-        return carry
-
-    lax.fori_loop(1, n - 1, gather_step, 0)
-
-    for piece in range(PIECES):
-
-        @pl.when(z == n - 1)
-        def _():
-            to_right(piece, 0).wait_recv()
-
-        @pl.when(z == 0)
-        def _():
-            to_left(piece, n - 1).wait_recv()
-
+    for piece in range(PIECES):
+        each_peer(lambda peer: gather_to(piece, peer, peer).wait_recv())
         for block in range(n):
             stack[block * rows : (block + 1) * rows, :] = blocks[piece, block].astype(F32)
         left_side = stack[...].astype(BF16)
@@ -294,98 +257,36 @@
         dfeat[part, long:, :] = tail
     lax.fori_loop(0, channels // lanes, channel_step, 0)
 
-    def pass_right(piece, block):
+    def scatter_to(piece, slot, peer):
         return pltpu.make_async_remote_copy(
-            src_ref=outgoing.at[piece, block],
-            dst_ref=from_left.at[piece, block],
-            send_sem=scatter_send.at[piece, block],
-            recv_sem=left_recv.at[piece, block],
-            device_id={"tp": z + 1},
+            src_ref=outgoing.at[piece, peer],
+            dst_ref=incoming.at[piece, slot],
+            send_sem=scatter_send.at[piece, peer],
+            recv_sem=scatter_recv.at[piece, slot],
+            device_id={"tp": peer},
             device_id_type=MESH,
         )
 
-    def pass_left(piece, block):
-        return pltpu.make_async_remote_copy(
-            src_ref=outgoing.at[piece, block],
-            dst_ref=from_right.at[piece, block],
-            send_sem=scatter_send.at[piece, block],
-            recv_sem=right_recv.at[piece, block],
-            device_id={"tp": z - 1},
-            device_id_type=MESH,
-        )
-
-    def begin(piece):
-        def step_of(step, carry):
-            far, near = n - 1 - step, step
-
-            @pl.when(z == 0)
-            def _():
-                outgoing[piece, far] = partial[piece, far].astype(BF16)
-                pass_right(piece, far).start()
-
-            @pl.when(z == n - 1)
-            def _():
-                outgoing[piece, near] = partial[piece, near].astype(BF16)
-                pass_left(piece, near).start()
-
-            return carry
-
-        lax.fori_loop(0, n - 1, step_of, 0)
-
-    def forward(piece):
-        def step_of(step, carry):
-            far, near = n - 1 - step, step
-
-            @pl.when((z > 0) & (z < far))
-            def _():
-                pass_right(piece, far).wait_recv()
-                outgoing[piece, far] = (
-                    from_left[piece, far].astype(F32) + partial[piece, far]
-                ).astype(BF16)
-                pass_right(piece, far).start()
-
-            @pl.when((z < n - 1) & (z > near))
-            def _():
-                pass_left(piece, near).wait_recv()
-                outgoing[piece, near] = (
-                    from_right[piece, near].astype(F32) + partial[piece, near]
-                ).astype(BF16)
-                pass_left(piece, near).start()
-
-            return carry
-
-        lax.fori_loop(0, n - 1, step_of, 0)
-
-    for piece in range(PIECES):
-        turned = jnp.zeros((cut, total), F32)
+    for piece in range(PIECES):
+        share = jnp.zeros((total, cut), F32)
         for part in range(3):
-            turned += lax.dot_general(
+            share += lax.dot_general(
+                dproj[part],
                 weight[part, piece * cut : (piece + 1) * cut, :],
-                dproj[part],
                 (((1,), (1,)), ((), ())),
                 preferred_element_type=F32,
             )
-        share = turned.T
         for block in range(n):
-            partial[piece, block] = share[block * rows : (block + 1) * rows]
-        begin(piece)
-        if piece > 0:
-            forward(piece - 1)
-    forward(PIECES - 1)
-
-    for piece in range(PIECES):
-
-        @pl.when(has_left)
-        def _():
-            pass_right(piece, z).wait_recv()
-            partial[piece, z] += from_left[piece, z].astype(F32)
-
-        @pl.when(has_right)
-        def _():
-            pass_left(piece, z).wait_recv()
-            partial[piece, z] += from_right[piece, z].astype(F32)
-
-        grad_tokens[:, piece * cut : (piece + 1) * cut] = partial[piece, z].astype(BF16)
+            outgoing[piece, block] = share[block * rows : (block + 1) * rows].astype(BF16)
+        each_peer(lambda peer: scatter_to(piece, z, peer).start())
+
+    for piece in range(PIECES):
+        incoming[piece, z] = outgoing[piece, z]
+        each_peer(lambda peer: scatter_to(piece, peer, peer).wait_recv())
+        summed = incoming[piece, 0].astype(F32)
+        for block in range(1, n):
+            summed += incoming[piece, block].astype(F32)
+        grad_tokens[:, piece * cut : (piece + 1) * cut] = summed.astype(BF16)
 
     @pl.when(has_before)
     def _():
@@ -396,24 +297,13 @@
     def _():
         last_rows.wait_send()
 
-    def drain(block, carry):
-        for piece in range(PIECES):
-
-            @pl.when(has_right & (block <= z))
-            def _():
-                to_right(piece, block).wait_send()
-
-            @pl.when(has_left & (block >= z))
-            def _():
-                to_left(piece, block).wait_send()
-
-            @pl.when(block != z)
-            def _():
-                pass_right(piece, block).wait_send()
-
-        return carry
-
-    lax.fori_loop(0, n, drain, 0)
+    for piece in range(PIECES):
+
+        def drain(peer):
+            gather_to(piece, z, peer).wait_send()
+            scatter_to(piece, z, peer).wait_send()
+
+        each_peer(drain)
 
 
 def local(n, n_ctx, tokens, proj_weight, feat_taps, inner_taps, grad_out):
@@ -449,13 +339,9 @@
             pltpu.VMEM((2, 3, HALO, channels), F32),
             pltpu.VMEM((HALO, channels), F32),
             pltpu.VMEM((HALO, channels), F32),
-            pltpu.VMEM((PIECES, n, rows, cut), F32),
-            pltpu.VMEM((PIECES, n, rows, cut), BF16),
             pltpu.VMEM((PIECES, n, rows, cut), BF16),
             pltpu.VMEM((PIECES, n, rows, cut), BF16),
             dma((PIECES, 3)),
-            dma((PIECES, n)),
-            dma((PIECES, n)),
             dma((PIECES, n)),
             dma((PIECES, n)),
             dma((PIECES, n)),
@@ -466,7 +352,7 @@
             dma((3,)),
         ],
         compiler_params=pltpu.CompilerParams(
-            collective_id=0, has_side_effects=True, vmem_limit_bytes=58 * 1024 * 1024
+            collective_id=0, has_side_effects=True, vmem_limit_bytes=50 * 1024 * 1024
         ),
         cost_estimate=pl.CostEstimate(
             flops=4 * total * width * 3 * channels,

time: 71.7 us -> 54.1 us (0.75); the launches traced: 71.6 us -> 53.2 us
  Pallas kernels: 67.7 us -> 47.9 us
  local copies, waits for them, and re-layouts: 3.2 us -> 4.67 us
    pallas_call x1, Pallas kernels: 67.7 us -> 47.9 us  [local(): pl.pallas_call(functools.partial(kernel, n, n_ctx), out_shape=(jax.ShapeD...]
    unnamed x2 -> x10, local copies, waits for them, and re-layouts: 3.2 us -> 4.67 us
where the time goes in v3:
time: 54.1 us; the launch traced here: 53.2 us
  Pallas kernels  47.9 us (89%)
  local copies, waits for them, and re-layouts  4.67 us (9%)
  between operations  0.65 us (1%)
    pallas_call x1, Pallas kernels, local(): pl.pallas_call(functools.partial(kernel, n, n_ctx), out_shape=(jax.ShapeD...  47.9 us
    unnamed x10, local copies, waits for them, and re-layouts  4.67 us

profile of v3, /device:TPU:4, one launch (start us, length us, event | category | flops | bytes accessed | tf_op | source)
XLA Modules:
  0.0 53.2 jit_solution(6074684664947138021)
XLA Ops:
  0.6 0.0 copy-start
  0.6 0.9 %copy-done = bf16[24,4096]{1,0:T(8,128)(2,1)S(1)} copy-done((bf16[24,4096]{1,0:T(8,128)(2,1)S(1)}, bf16[24,4096]{1,0:T(8,128)(2,1)}, u32[]{:S(2)}) %copy-start) | copy-done | bytes 196632
  1.6 0.0 copy-start.1
  1.6 0.9 %copy-done.1 = bf16[96,768]{1,0:T(8,128)(2,1)S(1)} copy-done((bf16[96,768]{1,0:T(8,128)(2,1)S(1)}, bf16[96,768]{1,0:T(8,128)(2,1)}, u32[]{:S(2)}) %copy-start.1) | copy-done | bytes 147480
  2.5 0.0 copy-start.2
  2.5 0.8 %copy-done.2 = f32[3,3,768]{2,1,0:T(4,128)S(1)} copy-done((f32[3,3,768]{2,1,0:T(4,128)S(1)}, f32[3,3,768]{2,1,0:T(4,128)}, u32[]{:S(2)}) %copy-start.2) | copy-done | bytes 27672
  3.2 0.0 copy-start.3
  3.2 0.7 %copy-done.3 = f32[7,768]{1,0:T(8,128)S(1)} copy-done((f32[7,768]{1,0:T(8,128)S(1)}, f32[7,768]{1,0:T(8,128)}, u32[]{:S(2)}) %copy-start.3) | copy-done | bytes 21528
  4.0 47.9 %shard_map.68 = (bf16[96,768]{1,0:T(8,128)(2,1)S(1)}, bf16[24,4096]{1,0:T(8,128)(2,1)S(1)}) custom-call(bf16[24,4096]{1,0:T(8,128)(2,1)S(1)} %copy-done, bf16[3,4096,768]{2,1,0:T(8,128)(2,1)} %bitcast.1, f32[3,3,768]{2,1,0:T(4,128)S(1)} %copy-done.2, f32[7,768]{1,0:T(8,128)S(1)} %copy-done.3, bf16[96,768]{1,0:T(8,128)(2,1)S(1)} %copy-done.1), custom_call_target="tpu_custom_call" | custom-call | flops 3623878656 | bytes 18874368 | tf_op jit(solution)/shard_map/pallas_call | solution.py:317
  51.9 0.7 %copy.9 = bf16[96,768]{1,0:T(8,128)(2,1)} copy(bf16[96,768]{1,0:T(8,128)(2,1)S(1)} %get-tuple-element.4) | data formatting | bytes 294912
  52.5 0.7 %copy.10 = bf16[24,4096]{1,0:T(8,128)(2,1)} copy(bf16[24,4096]{1,0:T(8,128)(2,1)S(1)} %get-tuple-element.5) | data formatting | bytes 393216
Async XLA Ops:
  0.6 0.9 %copy-start = (bf16[24,4096]{1,0:T(8,128)(2,1)S(1)}, bf16[24,4096]{1,0:T(8,128)(2,1)}, u32[]{:S(2)}) copy-start(bf16[24,4096]{1,0:T(8,128)(2,1)} %tokens.1) | copy-start | bytes 589828
  1.6 0.9 %copy-start.1 = (bf16[96,768]{1,0:T(8,128)(2,1)S(1)}, bf16[96,768]{1,0:T(8,128)(2,1)}, u32[]{:S(2)}) copy-start(bf16[96,768]{1,0:T(8,128)(2,1)} %grad_hbm.1) | copy-start | bytes 442372
  2.5 0.8 %copy-start.2 = (f32[3,3,768]{2,1,0:T(4,128)S(1)}, f32[3,3,768]{2,1,0:T(4,128)}, u32[]{:S(2)}) copy-start(f32[3,3,768]{2,1,0:T(4,128)} %feat_hbm.1) | copy-start | bytes 82948
  3.2 0.7 %copy-start.3 = (f32[7,768]{1,0:T(8,128)S(1)}, f32[7,768]{1,0:T(8,128)}, u32[]{:S(2)}) copy-start(f32[7,768]{1,0:T(8,128)} %inner_hbm.1) | copy-start | bytes 64516

commit v4 on v3

--- a/solution.py
+++ b/solution.py
@@ -11,6 +11,7 @@
 F32 = jnp.float32
 BF16 = jnp.bfloat16
 PIECES = 8
+GROUPS = ((0, 1), (2, 3), (4, 5), (6,), (7,))
 HALO = 8
 
 
@@ -42,9 +43,13 @@
     grad_halo,
     outgoing,
     incoming,
+    relay,
+    summed,
     weight_sem,
     gather_recv,
     gather_send,
+    forward_send,
+    relay_recv,
     scatter_recv,
     scatter_send,
     halo_send,
@@ -101,6 +106,16 @@
 
         lax.fori_loop(0, n - 1, visit, 0)
 
+    mate = z + 1 - 2 * lax.rem(z, 2)
+    even = lax.rem(z, 2) == 0
+
+    def faces(peer):
+        parity = lax.rem(peer, 2)
+        return ((peer > z) & (parity == 0)) | ((peer < z) & (parity == 1))
+
+    def is_relay_for(peer):
+        return (even & (peer < z)) | (jnp.logical_not(even) & (peer > z))
+
     def greet(here, axis, index):
         @pl.when(here)
         def _():
@@ -131,8 +146,26 @@
             device_id_type=MESH,
         )
 
+    def forward_to_mate(piece, block):
+        return pltpu.make_async_remote_copy(
+            src_ref=blocks.at[piece, block],
+            dst_ref=blocks.at[piece, block],
+            send_sem=forward_send.at[piece, block],
+            recv_sem=gather_recv.at[piece, block],
+            device_id={"tp": mate},
+            device_id_type=MESH,
+        )
+
+    def spread(piece):
+        def send(peer):
+            @pl.when((peer == mate) | faces(peer))
+            def _():
+                gather_to(piece, z, peer).start()
+
+        each_peer(send)
+
     for piece in range(PIECES):
-        each_peer(lambda peer: gather_to(piece, z, peer).start())
+        spread(piece)
 
     grad_copy = pltpu.make_async_remote_copy(
         src_ref=grad_edge,
@@ -147,19 +180,40 @@
     def _():
         grad_copy.start()
 
-    for piece in range(PIECES):
-        each_peer(lambda peer: gather_to(piece, peer, peer).wait_recv())
-        for block in range(n):
-            stack[block * rows : (block + 1) * rows, :] = blocks[piece, block].astype(F32)
-        left_side = stack[...].astype(BF16)
+    def collect(piece):
+        def take(peer):
+            @pl.when(is_relay_for(peer))
+            def _():
+                gather_to(piece, peer, peer).wait_recv()
+                forward_to_mate(piece, peer).start()
+
+        def take_rest(peer):
+            @pl.when(jnp.logical_not(is_relay_for(peer)))
+            def _():
+                gather_to(piece, peer, peer).wait_recv()
+
+        each_peer(take)
+        each_peer(take_rest)
+
+    for group in GROUPS:
+        for place, piece in enumerate(group):
+            collect(piece)
+            for block in range(n):
+                stack[block * rows : (block + 1) * rows, place * cut : (place + 1) * cut] = (
+                    blocks[piece, block].astype(F32)
+                )
+            for part in range(3):
+                weight_copy(piece, part).wait()
+        depth = len(group) * cut
+        left_side = stack[:, 0:depth].astype(BF16)
+        first = group[0] * cut
         for part in range(3):
-            weight_copy(piece, part).wait()
             product = jnp.dot(
                 left_side,
-                weight[part, piece * cut : (piece + 1) * cut, :],
+                weight[part, first : first + depth, :],
                 preferred_element_type=F32,
             )
-            if piece == 0:
+            if group[0] == 0:
                 ext[part, HALO : HALO + total, :] = product
             else:
                 ext[part, HALO : HALO + total, :] += product
@@ -267,6 +321,28 @@
             device_id_type=MESH,
         )
 
+    def relay_to_mate(piece, block):
+        return pltpu.make_async_remote_copy(
+            src_ref=outgoing.at[piece, block],
+            dst_ref=relay.at[piece, block],
+            send_sem=scatter_send.at[piece, block],
+            recv_sem=relay_recv.at[piece, block],
+            device_id={"tp": mate},
+            device_id_type=MESH,
+        )
+
+    def combine(piece):
+        def add(peer):
+            @pl.when(is_relay_for(peer))
+            def _():
+                relay_to_mate(piece, peer).wait_recv()
+                outgoing[piece, peer] = (
+                    outgoing[piece, peer].astype(F32) + relay[piece, peer].astype(F32)
+                ).astype(BF16)
+                scatter_to(piece, z, peer).start()
+
+        each_peer(add)
+
     for piece in range(PIECES):
         share = jnp.zeros((total, cut), F32)
         for part in range(3):
@@ -278,15 +354,30 @@
             )
         for block in range(n):
             outgoing[piece, block] = share[block * rows : (block + 1) * rows].astype(BF16)
-        each_peer(lambda peer: scatter_to(piece, z, peer).start())
+
+        def hand_over(peer):
+            @pl.when(jnp.logical_not(is_relay_for(peer)) & (peer != mate))
+            def _():
+                relay_to_mate(piece, peer).start()
+
+        each_peer(hand_over)
+        scatter_to(piece, z, mate).start()
+        if piece > 0:
+            combine(piece - 1)
+    combine(PIECES - 1)
 
     for piece in range(PIECES):
-        incoming[piece, z] = outgoing[piece, z]
-        each_peer(lambda peer: scatter_to(piece, peer, peer).wait_recv())
-        summed = incoming[piece, 0].astype(F32)
-        for block in range(1, n):
-            summed += incoming[piece, block].astype(F32)
-        grad_tokens[:, piece * cut : (piece + 1) * cut] = summed.astype(BF16)
+        scatter_to(piece, mate, mate).wait_recv()
+        summed[...] = outgoing[piece, z].astype(F32) + incoming[piece, mate].astype(F32)
+
+        def gain(peer):
+            @pl.when(faces(peer) & (peer != mate))
+            def _():
+                scatter_to(piece, peer, peer).wait_recv()
+                summed[...] += incoming[piece, peer].astype(F32)
+
+        each_peer(gain)
+        grad_tokens[:, piece * cut : (piece + 1) * cut] = summed[...].astype(BF16)
 
     @pl.when(has_before)
     def _():
@@ -300,7 +391,14 @@
     for piece in range(PIECES):
 
         def drain(peer):
-            gather_to(piece, z, peer).wait_send()
+            @pl.when((peer == mate) | faces(peer))
+            def _():
+                gather_to(piece, z, peer).wait_send()
+
+            @pl.when(is_relay_for(peer))
+            def _():
+                forward_to_mate(piece, peer).wait_send()
+
             scatter_to(piece, z, peer).wait_send()
 
         each_peer(drain)
@@ -320,7 +418,7 @@
             jax.ShapeDtypeStruct((total, channels), BF16),
             jax.ShapeDtypeStruct((rows, width), BF16),
         ),
-        in_specs=[pl.BlockSpec(memory_space=pl.ANY)] * 5,
+        in_specs=[pl.BlockSpec(memory_space=pltpu.HBM)] * 5,
         out_specs=(vmem, vmem),
         scratch_shapes=[
             pltpu.VMEM(feat_taps.shape, F32),
@@ -328,7 +426,7 @@
             pltpu.VMEM((total, channels), BF16),
             pltpu.VMEM((3, width, channels), BF16),
             pltpu.VMEM((PIECES, n, rows, cut), BF16),
-            pltpu.VMEM((total, cut), F32),
+            pltpu.VMEM((total, 2 * cut), F32),
             pltpu.VMEM((3, long, channels), F32),
             pltpu.VMEM((total + HALO, channels), F32),
             pltpu.VMEM((long, 128), F32),
@@ -341,7 +439,11 @@
             pltpu.VMEM((HALO, channels), F32),
             pltpu.VMEM((PIECES, n, rows, cut), BF16),
             pltpu.VMEM((PIECES, n, rows, cut), BF16),
+            pltpu.VMEM((PIECES, n, rows, cut), BF16),
+            pltpu.VMEM((rows, cut), F32),
             dma((PIECES, 3)),
+            dma((PIECES, n)),
+            dma((PIECES, n)),
             dma((PIECES, n)),
             dma((PIECES, n)),
             dma((PIECES, n)),

time: 54.1 us -> 49.1 us (0.908)
  Pallas kernels: 47.9 us -> 42.9 us
    pallas_call x1, Pallas kernels: 47.9 us -> 42.9 us  [local(): pl.pallas_call(functools.partial(kernel, n, n_ctx), out_shape=(jax.ShapeD...]
where the time goes in v4:
time: 49.1 us; the launch traced here: 48.3 us
  Pallas kernels  42.9 us (87%)
  local copies, waits for them, and re-layouts  4.67 us (10%)
  between operations  0.65 us (1%)
    pallas_call x1, Pallas kernels, local(): pl.pallas_call(functools.partial(kernel, n, n_ctx), out_shape=(jax.ShapeD...  42.9 us
    unnamed x10, local copies, waits for them, and re-layouts  4.67 us

profile of v4, /device:TPU:4, one launch (start us, length us, event | category | flops | bytes accessed | tf_op | source)
XLA Modules:
  0.0 48.3 jit_solution(11042444350457556949)
XLA Ops:
  0.6 0.0 copy-start
  0.6 0.9 %copy-done = bf16[24,4096]{1,0:T(8,128)(2,1)S(1)} copy-done((bf16[24,4096]{1,0:T(8,128)(2,1)S(1)}, bf16[24,4096]{1,0:T(8,128)(2,1)}, u32[]{:S(2)}) %copy-start) | copy-done | bytes 196632
  1.6 0.0 copy-start.1
  1.6 0.9 %copy-done.1 = bf16[96,768]{1,0:T(8,128)(2,1)S(1)} copy-done((bf16[96,768]{1,0:T(8,128)(2,1)S(1)}, bf16[96,768]{1,0:T(8,128)(2,1)}, u32[]{:S(2)}) %copy-start.1) | copy-done | bytes 147480
  2.5 0.0 copy-start.2
  2.5 0.8 %copy-done.2 = f32[3,3,768]{2,1,0:T(4,128)S(1)} copy-done((f32[3,3,768]{2,1,0:T(4,128)S(1)}, f32[3,3,768]{2,1,0:T(4,128)}, u32[]{:S(2)}) %copy-start.2) | copy-done | bytes 27672
  3.2 0.0 copy-start.3
  3.2 0.7 %copy-done.3 = f32[7,768]{1,0:T(8,128)S(1)} copy-done((f32[7,768]{1,0:T(8,128)S(1)}, f32[7,768]{1,0:T(8,128)}, u32[]{:S(2)}) %copy-start.3) | copy-done | bytes 21528
  4.0 42.9 %shard_map.68 = (bf16[96,768]{1,0:T(8,128)(2,1)S(1)}, bf16[24,4096]{1,0:T(8,128)(2,1)S(1)}) custom-call(bf16[24,4096]{1,0:T(8,128)(2,1)S(1)} %copy-done, bf16[3,4096,768]{2,1,0:T(8,128)(2,1)} %bitcast.1, f32[3,3,768]{2,1,0:T(4,128)S(1)} %copy-done.2, f32[7,768]{1,0:T(8,128)S(1)} %copy-done.3, bf16[96,768]{1,0:T(8,128)(2,1)S(1)} %copy-done.1), custom_call_target="tpu_custom_call" | custom-call | flops 3623878656 | bytes 18874368 | tf_op jit(solution)/shard_map/pallas_call | solution.py:415
  46.9 0.7 %copy.9 = bf16[96,768]{1,0:T(8,128)(2,1)} copy(bf16[96,768]{1,0:T(8,128)(2,1)S(1)} %get-tuple-element.4) | data formatting | bytes 294912
  47.6 0.7 %copy.10 = bf16[24,4096]{1,0:T(8,128)(2,1)} copy(bf16[24,4096]{1,0:T(8,128)(2,1)S(1)} %get-tuple-element.5) | data formatting | bytes 393216
Async XLA Ops:
  0.6 0.9 %copy-start = (bf16[24,4096]{1,0:T(8,128)(2,1)S(1)}, bf16[24,4096]{1,0:T(8,128)(2,1)}, u32[]{:S(2)}) copy-start(bf16[24,4096]{1,0:T(8,128)(2,1)} %tokens.1) | copy-start | bytes 589828
  1.6 0.9 %copy-start.1 = (bf16[96,768]{1,0:T(8,128)(2,1)S(1)}, bf16[96,768]{1,0:T(8,128)(2,1)}, u32[]{:S(2)}) copy-start(bf16[96,768]{1,0:T(8,128)(2,1)} %grad_hbm.1) | copy-start | bytes 442372
  2.5 0.8 %copy-start.2 = (f32[3,3,768]{2,1,0:T(4,128)S(1)}, f32[3,3,768]{2,1,0:T(4,128)}, u32[]{:S(2)}) copy-start(f32[3,3,768]{2,1,0:T(4,128)} %feat_hbm.1) | copy-start | bytes 82948
  3.2 0.7 %copy-start.3 = (f32[7,768]{1,0:T(8,128)S(1)}, f32[7,768]{1,0:T(8,128)}, u32[]{:S(2)}) copy-start(f32[7,768]{1,0:T(8,128)} %inner_hbm.1) | copy-start | bytes 64516

commit v5 on v4

--- a/solution.py
+++ b/solution.py
@@ -23,6 +23,8 @@
     feat_hbm,
     inner_hbm,
     grad_hbm,
+    gated_hbm,
+    grad_tokens_hbm,
     gated,
     grad_tokens,
     feat_taps,
@@ -61,6 +63,7 @@
     ctx = lax.axis_index("ctx")
     rows, width = tokens.shape
     total, channels = gated.shape
+    edge_rows = 2 * HALO
     cut = width // PIECES
 
     def weight_copy(piece, part):
@@ -128,13 +131,18 @@
     greet(has_before, "ctx", ctx - 1)
     greet(has_after, "ctx", ctx + 1)
 
-    for copy in own + small:
-        copy.wait()
-    grads[0:total, :] = grad_out[...].astype(F32)
-    grad_edge[...] = grads[0:HALO, :]
-
     peers = n - 1 + has_before.astype(jnp.int32) + has_after.astype(jnp.int32)
     pl.semaphore_wait(barrier, peers)
+
+    def send_own(piece, peer):
+        return pltpu.make_async_remote_copy(
+            src_ref=tokens.at[:, pl.ds(piece * cut, cut)],
+            dst_ref=blocks.at[piece, z],
+            send_sem=gather_send.at[piece, peer],
+            recv_sem=gather_recv.at[piece, z],
+            device_id={"tp": peer},
+            device_id_type=MESH,
+        )
 
     def gather_to(piece, block, peer):
         return pltpu.make_async_remote_copy(
@@ -160,12 +168,17 @@
         def send(peer):
             @pl.when((peer == mate) | faces(peer))
             def _():
-                gather_to(piece, z, peer).start()
+                send_own(piece, peer).start()
 
         each_peer(send)
 
     for piece in range(PIECES):
         spread(piece)
+
+    for copy in own + small:
+        copy.wait()
+    grads[0:total, :] = grad_out[...].astype(F32)
+    grad_edge[...] = grads[0:HALO, :]
 
     grad_copy = pltpu.make_async_remote_copy(
         src_ref=grad_edge,
@@ -242,32 +255,11 @@
     def _():
         last_rows.start()
 
-    @pl.when(has_after)
-    def _():
-        grad_copy.wait_recv()
-        grads[total : total + HALO, :] = grad_halo[...]
-        first_rows.wait_recv()
-        ext[:, HALO + total :, :] = halo[0]
-
-    @pl.when(ctx == n_ctx - 1)
-    def _():
-        grads[total : total + HALO, :] = jnp.zeros((HALO, channels), F32)
-        ext[:, HALO + total :, :] = jnp.zeros((3, HALO, channels), F32)
-
-    @pl.when(has_before)
-    def _():
-        last_rows.wait_recv()
-        ext[:, 0:HALO, :] = halo[1]
-
-    @pl.when(ctx == 0)
-    def _():
-        ext[:, 0:HALO, :] = jnp.zeros((3, HALO, channels), F32)
-
-    long = total + HALO
-    lanes = 128
-
-    def channel_step(index, carry):
-        at = pl.ds(pl.multiple_of(index * lanes, lanes), lanes)
+    for scratch in (mix, dinner, dfeat):
+        scratch[...] = jnp.zeros(scratch.shape, F32)
+
+    def convolve(top, count, at):
+        long = count + HALO
 
         def conv(part, start):
             terms = feat_taps[part, 0:1, at] * ext[part, start : start + long, at]
@@ -278,38 +270,69 @@
                 )
             return terms
 
-        query = conv(0, HALO)
-        dinner[0:long, :] = grads[:, at] * query
-        key = conv(1, 2)
-        value = conv(2, 2)
-        mix[0:long, :] = key * value
-        dfeat[1, 0:long, :] = value
-        dfeat[2, 0:long, :] = key
-        inner = inner_taps[0:1, at] * mix[6 : 6 + long, :]
+        cotangent = grads[top : top + long, at]
+        query = conv(0, top + HALO)
+        dinner[0:long, at] = cotangent * query
+        key = conv(1, top + 2)
+        value = conv(2, top + 2)
+        mix[0:long, at] = key * value
+        dfeat[1, 0:long, at] = value
+        dfeat[2, 0:long, at] = key
+        inner = inner_taps[0:1, at] * mix[6 : 6 + long, at]
         for tap in range(1, 7):
-            inner += inner_taps[tap : tap + 1, at] * mix[6 - tap : 6 - tap + long, :]
-        gated[:, at] = (query * inner)[0:total].astype(BF16)
-        dfeat[0, 0:long, :] = grads[:, at] * inner
-        dmix = inner_taps[0:1, at] * dinner[0:long, :]
+            inner += inner_taps[tap : tap + 1, at] * mix[6 - tap : 6 - tap + long, at]
+        gated[top : top + count, at] = (query * inner)[0:count].astype(BF16)
+        dfeat[0, 0:long, at] = cotangent * inner
+        dmix = inner_taps[0:1, at] * dinner[0:long, at]
         for tap in range(1, 7):
-            dmix += inner_taps[tap : tap + 1, at] * dinner[tap : tap + long, :]
-        dkey = dmix * dfeat[1, 6 : 6 + long, :]
-        dvalue = dmix * dfeat[2, 6 : 6 + long, :]
-        dfeat[1, 0:long, :] = dkey
-        dfeat[2, 0:long, :] = dvalue
+            dmix += inner_taps[tap : tap + 1, at] * dinner[tap : tap + long, at]
+        dkey = dmix * dfeat[1, 6 : 6 + long, at]
+        dvalue = dmix * dfeat[2, 6 : 6 + long, at]
+        dfeat[1, 0:long, at] = dkey
+        dfeat[2, 0:long, at] = dvalue
         for part in range(3):
-            series = feat_taps[part, 0:1, at] * dfeat[part, 0:total, :]
+            series = feat_taps[part, 0:1, at] * dfeat[part, 0:count, at]
             for tap in range(1, 3):
-                series += feat_taps[part, tap : tap + 1, at] * dfeat[part, tap : tap + total, :]
-            dproj[part, :, at] = series.astype(BF16)
-        return carry
-
-    tail = jnp.zeros((HALO, lanes), F32)
-    mix[long:, :] = tail
-    dinner[long:, :] = tail
-    for part in range(3):
-        dfeat[part, long:, :] = tail
-    lax.fori_loop(0, channels // lanes, channel_step, 0)
+                series += feat_taps[part, tap : tap + 1, at] * dfeat[part, tap : tap + count, at]
+            dproj[part, top : top + count, at] = series.astype(BF16)
+
+    def each_lanes(act):
+        def visit(index, carry):
+            act(pl.ds(pl.multiple_of(index * 128, 128), 128))
+            return carry
+
+        lax.fori_loop(0, channels // 128, visit, 0)
+
+    each_lanes(lambda at: convolve(edge_rows, total - 2 * edge_rows, at))
+
+    @pl.when(has_after)
+    def _():
+        grad_copy.wait_recv()
+        grads[total : total + HALO, :] = grad_halo[...]
+        first_rows.wait_recv()
+        ext[:, HALO + total :, :] = halo[0]
+
+    @pl.when(ctx == n_ctx - 1)
+    def _():
+        grads[total : total + HALO, :] = jnp.zeros((HALO, channels), F32)
+        ext[:, HALO + total :, :] = jnp.zeros((3, HALO, channels), F32)
+
+    @pl.when(has_before)
+    def _():
+        last_rows.wait_recv()
+        ext[:, 0:HALO, :] = halo[1]
+
+    @pl.when(ctx == 0)
+    def _():
+        ext[:, 0:HALO, :] = jnp.zeros((3, HALO, channels), F32)
+
+    def edges(at):
+        convolve(0, edge_rows, at)
+        convolve(total - edge_rows, edge_rows, at)
+
+    each_lanes(edges)
+    gated_copy = pltpu.make_async_copy(gated, gated_hbm, small_sem.at[3])
+    gated_copy.start()
 
     def scatter_to(piece, slot, peer):
         return pltpu.make_async_remote_copy(
@@ -366,6 +389,13 @@
             combine(piece - 1)
     combine(PIECES - 1)
 
+    def result_copy(piece):
+        return pltpu.make_async_copy(
+            grad_tokens.at[piece],
+            grad_tokens_hbm.at[:, pl.ds(piece * cut, cut)],
+            token_sem.at[piece],
+        )
+
     for piece in range(PIECES):
         scatter_to(piece, mate, mate).wait_recv()
         summed[...] = outgoing[piece, z].astype(F32) + incoming[piece, mate].astype(F32)
@@ -377,7 +407,8 @@
                 summed[...] += incoming[piece, peer].astype(F32)
 
         each_peer(gain)
-        grad_tokens[:, piece * cut : (piece + 1) * cut] = summed[...].astype(BF16)
+        grad_tokens[piece] = summed[...].astype(BF16)
+        result_copy(piece).start()
 
     @pl.when(has_before)
     def _():
@@ -393,7 +424,7 @@
         def drain(peer):
             @pl.when((peer == mate) | faces(peer))
             def _():
-                gather_to(piece, z, peer).wait_send()
+                send_own(piece, peer).wait_send()
 
             @pl.when(is_relay_for(peer))
             def _():
@@ -402,6 +433,9 @@
             scatter_to(piece, z, peer).wait_send()
 
         each_peer(drain)
+        result_copy(piece).wait()
+
+    gated_copy.wait()
 
 
 def local(n, n_ctx, tokens, proj_weight, feat_taps, inner_taps, grad_out):
@@ -409,7 +443,7 @@
     total, channels = grad_out.shape
     cut = width // PIECES
     weight = jnp.transpose(proj_weight, (1, 0, 2))
-    vmem = pl.BlockSpec(memory_space=pltpu.VMEM)
+    anywhere = pl.BlockSpec(memory_space=pl.ANY)
     dma = pltpu.SemaphoreType.DMA
     long = total + 2 * HALO
     return pl.pallas_call(
@@ -418,9 +452,11 @@
             jax.ShapeDtypeStruct((total, channels), BF16),
             jax.ShapeDtypeStruct((rows, width), BF16),
         ),
-        in_specs=[pl.BlockSpec(memory_space=pltpu.HBM)] * 5,
-        out_specs=(vmem, vmem),
+        in_specs=[anywhere] * 5,
+        out_specs=(anywhere, anywhere),
         scratch_shapes=[
+            pltpu.VMEM((total, channels), BF16),
+            pltpu.VMEM((PIECES, rows, cut), BF16),
             pltpu.VMEM(feat_taps.shape, F32),
             pltpu.VMEM(inner_taps.shape, F32),
             pltpu.VMEM((total, channels), BF16),
@@ -429,9 +465,9 @@
             pltpu.VMEM((total, 2 * cut), F32),
             pltpu.VMEM((3, long, channels), F32),
             pltpu.VMEM((total + HALO, channels), F32),
-            pltpu.VMEM((long, 128), F32),
-            pltpu.VMEM((long, 128), F32),
-            pltpu.VMEM((3, long, 128), F32),
+            pltpu.VMEM((long, channels), F32),
+            pltpu.VMEM((long, channels), F32),
+            pltpu.VMEM((3, long, channels), F32),
             pltpu.VMEM((3, total, channels), BF16),
             pltpu.VMEM((2, 3, HALO, channels), F32),
             pltpu.VMEM((2, 3, HALO, channels), F32),
@@ -451,10 +487,10 @@
             dma((3,)),
             dma((3,)),
             dma((PIECES,)),
-            dma((3,)),
+            dma((4,)),
         ],
         compiler_params=pltpu.CompilerParams(
-            collective_id=0, has_side_effects=True, vmem_limit_bytes=50 * 1024 * 1024
+            collective_id=0, has_side_effects=True, vmem_limit_bytes=56 * 1024 * 1024
         ),
         cost_estimate=pl.CostEstimate(
             flops=4 * total * width * 3 * channels,

time: 49.1 us -> 47.3 us (0.963)
  local copies, waits for them, and re-layouts: 4.67 us -> 3.2 us
    unnamed x10 -> x2, local copies, waits for them, and re-layouts: 4.67 us -> 3.2 us
where the time goes in v5:
time: 47.3 us; the launch traced here: 46.6 us
  Pallas kernels  42.7 us (90%)
  local copies, waits for them, and re-layouts  3.2 us (7%)
  between operations  0.64 us (1%)
    pallas_call x1, Pallas kernels, local(): pl.pallas_call(functools.partial(kernel, n, n_ctx), out_shape=(jax.ShapeD...  42.7 us
    unnamed x2, local copies, waits for them, and re-layouts  3.2 us

profile of v5, /device:TPU:4, one launch (start us, length us, event | category | flops | bytes accessed | tf_op | source)
XLA Modules:
  0.0 46.6 jit_solution(2430959358142891809)
XLA Ops:
  0.6 42.7 %shard_map.68 = (bf16[96,768]{1,0:T(8,128)(2,1)}, bf16[24,4096]{1,0:T(8,128)(2,1)}) custom-call(bf16[24,4096]{1,0:T(8,128)(2,1)} %tokens.1, bf16[3,4096,768]{2,1,0:T(8,128)(2,1)} %bitcast.1, f32[3,3,768]{2,1,0:T(4,128)} %feat_hbm.1, f32[7,768]{1,0:T(8,128)} %inner_hbm.1, bf16[96,768]{1,0:T(8,128)(2,1)} %grad_hbm.1), custom_call_target="tpu_custom_call" | custom-call | flops 3623878656 | bytes 18874368 | tf_op jit(solution)/shard_map/pallas_call | solution.py:449
  43.4 1.6 %copy.9 = bf16[96,768]{1,0:T(8,128)(2,1)} copy(bf16[96,768]{1,0:T(8,128)(2,1)} %get-tuple-element.4) | data formatting | bytes 294912
  45.0 1.6 %copy.10 = bf16[24,4096]{1,0:T(8,128)(2,1)} copy(bf16[24,4096]{1,0:T(8,128)(2,1)} %get-tuple-element.5) | data formatting | bytes 393216

commit v6 on v5

--- a/solution.py
+++ b/solution.py
@@ -84,12 +84,6 @@
             ((grad_hbm, grad_out), (feat_hbm, feat_taps), (inner_hbm, inner_taps))
         )
     ]
-    for copy in own + small:
-        copy.start()
-    for piece in range(PIECES):
-        for part in range(3):
-            weight_copy(piece, part).start()
-
     has_before, has_after = ctx > 0, ctx < n_ctx - 1
     barrier = pltpu.get_barrier_semaphore()
 
@@ -107,7 +101,11 @@
 
             return carry
 
-        lax.fori_loop(0, n - 1, visit, 0)
+        if n <= 8:
+            for index in range(n - 1):
+                visit(index, 0)
+        else:
+            lax.fori_loop(0, n - 1, visit, 0)
 
     mate = z + 1 - 2 * lax.rem(z, 2)
     even = lax.rem(z, 2) == 0
@@ -130,6 +128,11 @@
     each_peer(greet_peer)
     greet(has_before, "ctx", ctx - 1)
     greet(has_after, "ctx", ctx + 1)
+
+    for copy in own + small:
+        copy.start()
+    for part in range(3):
+        weight_copy(0, part).start()
 
     peers = n - 1 + has_before.astype(jnp.int32) + has_after.astype(jnp.int32)
     pl.semaphore_wait(barrier, peers)
@@ -174,6 +177,10 @@
 
     for piece in range(PIECES):
         spread(piece)
+
+    for piece in range(1, PIECES):
+        for part in range(3):
+            weight_copy(piece, part).start()
 
     for copy in own + small:
         copy.wait()
@@ -389,6 +396,30 @@
             combine(piece - 1)
     combine(PIECES - 1)
 
+    @pl.when(has_before)
+    def _():
+        grad_copy.wait_send()
+        first_rows.wait_send()
+
+    @pl.when(has_after)
+    def _():
+        last_rows.wait_send()
+
+    for piece in range(PIECES):
+
+        def drain(peer):
+            @pl.when((peer == mate) | faces(peer))
+            def _():
+                send_own(piece, peer).wait_send()
+
+            @pl.when(is_relay_for(peer))
+            def _():
+                forward_to_mate(piece, peer).wait_send()
+
+            scatter_to(piece, z, peer).wait_send()
+
+        each_peer(drain)
+
     def result_copy(piece):
         return pltpu.make_async_copy(
             grad_tokens.at[piece],
@@ -410,29 +441,7 @@
         grad_tokens[piece] = summed[...].astype(BF16)
         result_copy(piece).start()
 
-    @pl.when(has_before)
-    def _():
-        grad_copy.wait_send()
-        first_rows.wait_send()
-
-    @pl.when(has_after)
-    def _():
-        last_rows.wait_send()
-
     for piece in range(PIECES):
-
-        def drain(peer):
-            @pl.when((peer == mate) | faces(peer))
-            def _():
-                send_own(piece, peer).wait_send()
-
-            @pl.when(is_relay_for(peer))
-            def _():
-                forward_to_mate(piece, peer).wait_send()
-
-            scatter_to(piece, z, peer).wait_send()
-
-        each_peer(drain)
         result_copy(piece).wait()
 
     gated_copy.wait()

time: 47.3 us -> 46.9 us (level)
  Pallas kernels: 42.7 us -> 42.1 us
    pallas_call x1, Pallas kernels: 42.7 us -> 42.1 us  [local(): pl.pallas_call(functools.partial(kernel, n, n_ctx), out_shape=(jax.ShapeD...]
where the time goes in v6:
time: 46.9 us; the launch traced here: 46 us
  Pallas kernels  42.1 us (90%)
  local copies, waits for them, and re-layouts  3.2 us (7%)
  between operations  0.64 us (1%)
    pallas_call x1, Pallas kernels, local(): pl.pallas_call(functools.partial(kernel, n, n_ctx), out_shape=(jax.ShapeD...  42.1 us
    unnamed x2, local copies, waits for them, and re-layouts  3.2 us

profile of v6, /device:TPU:4, one launch (start us, length us, event | category | flops | bytes accessed | tf_op | source)
XLA Modules:
  0.0 46.0 jit_solution(12945177987096801305)
XLA Ops:
  0.6 42.1 %shard_map.68 = (bf16[96,768]{1,0:T(8,128)(2,1)}, bf16[24,4096]{1,0:T(8,128)(2,1)}) custom-call(bf16[24,4096]{1,0:T(8,128)(2,1)} %tokens.1, bf16[3,4096,768]{2,1,0:T(8,128)(2,1)} %bitcast.1, f32[3,3,768]{2,1,0:T(4,128)} %feat_hbm.1, f32[7,768]{1,0:T(8,128)} %inner_hbm.1, bf16[96,768]{1,0:T(8,128)(2,1)} %grad_hbm.1), custom_call_target="tpu_custom_call" | custom-call | flops 3623878656 | bytes 18874368 | tf_op jit(solution)/shard_map/pallas_call | solution.py:458
  42.8 1.6 %copy.9 = bf16[96,768]{1,0:T(8,128)(2,1)} copy(bf16[96,768]{1,0:T(8,128)(2,1)} %get-tuple-element.4) | data formatting | bytes 294912
  44.4 1.6 %copy.10 = bf16[24,4096]{1,0:T(8,128)(2,1)} copy(bf16[24,4096]{1,0:T(8,128)(2,1)} %get-tuple-element.5) | data formatting | bytes 393216

commit v7 on v6

--- a/solution.py
+++ b/solution.py
@@ -12,6 +12,8 @@
 BF16 = jnp.bfloat16
 PIECES = 8
 GROUPS = ((0, 1), (2, 3), (4, 5), (6,), (7,))
+RELAYED_GATHER = 4
+RELAYED_SCATTER = 6
 HALO = 8
 
 
@@ -173,7 +175,10 @@
             def _():
                 send_own(piece, peer).start()
 
-        each_peer(send)
+        if piece < RELAYED_GATHER:
+            each_peer(send)
+        else:
+            each_peer(lambda peer: send_own(piece, peer).start())
 
     for piece in range(PIECES):
         spread(piece)
@@ -212,8 +217,11 @@
             def _():
                 gather_to(piece, peer, peer).wait_recv()
 
-        each_peer(take)
-        each_peer(take_rest)
+        if piece < RELAYED_GATHER:
+            each_peer(take)
+            each_peer(take_rest)
+        else:
+            each_peer(lambda peer: gather_to(piece, peer, peer).wait_recv())
 
     for group in GROUPS:
         for place, piece in enumerate(group):
@@ -390,11 +398,13 @@
             def _():
                 relay_to_mate(piece, peer).start()
 
-        each_peer(hand_over)
-        scatter_to(piece, z, mate).start()
-        if piece > 0:
+        if piece < RELAYED_SCATTER:
+            each_peer(hand_over)
+            scatter_to(piece, z, mate).start()
+        else:
+            each_peer(lambda peer: scatter_to(piece, z, peer).start())
+        if 0 < piece <= RELAYED_SCATTER:
             combine(piece - 1)
-    combine(PIECES - 1)
 
     @pl.when(has_before)
     def _():
@@ -408,14 +418,18 @@
     for piece in range(PIECES):
 
         def drain(peer):
-            @pl.when((peer == mate) | faces(peer))
-            def _():
+            if piece < RELAYED_GATHER:
+
+                @pl.when((peer == mate) | faces(peer))
+                def _():
+                    send_own(piece, peer).wait_send()
+
+                @pl.when(is_relay_for(peer))
+                def _():
+                    forward_to_mate(piece, peer).wait_send()
+
+            else:
                 send_own(piece, peer).wait_send()
-
-            @pl.when(is_relay_for(peer))
-            def _():
-                forward_to_mate(piece, peer).wait_send()
-
             scatter_to(piece, z, peer).wait_send()
 
         each_peer(drain)
@@ -432,7 +446,9 @@
         summed[...] = outgoing[piece, z].astype(F32) + incoming[piece, mate].astype(F32)
 
         def gain(peer):
-            @pl.when(faces(peer) & (peer != mate))
+            sends = faces(peer) if piece < RELAYED_SCATTER else peer != mate
+
+            @pl.when(sends)
             def _():
                 scatter_to(piece, peer, peer).wait_recv()
                 summed[...] += incoming[piece, peer].astype(F32)

time: 46.9 us -> 49.3 us (1.051); the launches traced: 46 us -> 49.2 us
  Pallas kernels: 42.1 us -> 45.3 us
    pallas_call x1, Pallas kernels: 42.1 us -> 45.3 us  [local(): pl.pallas_call(functools.partial(kernel, n, n_ctx), out_shape=(jax.ShapeD...]
where the time goes in v7:
time: 49.3 us; the launch traced here: 49.2 us
  Pallas kernels  45.3 us (92%)
  local copies, waits for them, and re-layouts  3.2 us (6%)
  between operations  0.64 us (1%)
    pallas_call x1, Pallas kernels, local(): pl.pallas_call(functools.partial(kernel, n, n_ctx), out_shape=(jax.ShapeD...  45.3 us
    unnamed x2, local copies, waits for them, and re-layouts  3.2 us

profile of v7, /device:TPU:4, one launch (start us, length us, event | category | flops | bytes accessed | tf_op | source)
XLA Modules:
  0.0 49.2 jit_solution(14983820519625976850)
XLA Ops:
  0.6 45.3 %shard_map.68 = (bf16[96,768]{1,0:T(8,128)(2,1)}, bf16[24,4096]{1,0:T(8,128)(2,1)}) custom-call(bf16[24,4096]{1,0:T(8,128)(2,1)} %tokens.1, bf16[3,4096,768]{2,1,0:T(8,128)(2,1)} %bitcast.1, f32[3,3,768]{2,1,0:T(4,128)} %feat_hbm.1, f32[7,768]{1,0:T(8,128)} %inner_hbm.1, bf16[96,768]{1,0:T(8,128)(2,1)} %grad_hbm.1), custom_call_target="tpu_custom_call" | custom-call | flops 3623878656 | bytes 18874368 | tf_op jit(solution)/shard_map/pallas_call | solution.py:474
  46.0 1.6 %copy.9 = bf16[96,768]{1,0:T(8,128)(2,1)} copy(bf16[96,768]{1,0:T(8,128)(2,1)} %get-tuple-element.4) | data formatting | bytes 294912
  47.5 1.6 %copy.10 = bf16[24,4096]{1,0:T(8,128)(2,1)} copy(bf16[24,4096]{1,0:T(8,128)(2,1)} %get-tuple-element.5) | data formatting | bytes 393216

commit v8 on v6

--- a/solution.py
+++ b/solution.py
@@ -265,7 +265,7 @@
     for scratch in (mix, dinner, dfeat):
         scratch[...] = jnp.zeros(scratch.shape, F32)
 
-    def convolve(top, count, at):
+    def convolve(top, count, at, base=0):
         long = count + HALO
 
         def conv(part, start):
@@ -279,28 +279,28 @@
 
         cotangent = grads[top : top + long, at]
         query = conv(0, top + HALO)
-        dinner[0:long, at] = cotangent * query
+        dinner[base : base + long, at] = cotangent * query
         key = conv(1, top + 2)
         value = conv(2, top + 2)
-        mix[0:long, at] = key * value
-        dfeat[1, 0:long, at] = value
-        dfeat[2, 0:long, at] = key
-        inner = inner_taps[0:1, at] * mix[6 : 6 + long, at]
+        mix[base : base + long, at] = key * value
+        dfeat[1, base : base + long, at] = value
+        dfeat[2, base : base + long, at] = key
+        inner = inner_taps[0:1, at] * mix[base + 6 : base + 6 + long, at]
         for tap in range(1, 7):
-            inner += inner_taps[tap : tap + 1, at] * mix[6 - tap : 6 - tap + long, at]
+            inner += inner_taps[tap : tap + 1, at] * mix[base + 6 - tap : base + 6 - tap + long, at]
         gated[top : top + count, at] = (query * inner)[0:count].astype(BF16)
-        dfeat[0, 0:long, at] = cotangent * inner
-        dmix = inner_taps[0:1, at] * dinner[0:long, at]
+        dfeat[0, base : base + long, at] = cotangent * inner
+        dmix = inner_taps[0:1, at] * dinner[base : base + long, at]
         for tap in range(1, 7):
-            dmix += inner_taps[tap : tap + 1, at] * dinner[tap : tap + long, at]
-        dkey = dmix * dfeat[1, 6 : 6 + long, at]
-        dvalue = dmix * dfeat[2, 6 : 6 + long, at]
-        dfeat[1, 0:long, at] = dkey
-        dfeat[2, 0:long, at] = dvalue
+            dmix += inner_taps[tap : tap + 1, at] * dinner[base + tap : base + tap + long, at]
+        dkey = dmix * dfeat[1, base + 6 : base + 6 + long, at]
+        dvalue = dmix * dfeat[2, base + 6 : base + 6 + long, at]
+        dfeat[1, base : base + long, at] = dkey
+        dfeat[2, base : base + long, at] = dvalue
         for part in range(3):
-            series = feat_taps[part, 0:1, at] * dfeat[part, 0:count, at]
+            series = feat_taps[part, 0:1, at] * dfeat[part, base : base + count, at]
             for tap in range(1, 3):
-                series += feat_taps[part, tap : tap + 1, at] * dfeat[part, tap : tap + count, at]
+                series += feat_taps[part, tap : tap + 1, at] * dfeat[part, base + tap : base + tap + count, at]
             dproj[part, top : top + count, at] = series.astype(BF16)
 
     def each_lanes(act):
@@ -333,11 +333,11 @@
     def _():
         ext[:, 0:HALO, :] = jnp.zeros((3, HALO, channels), F32)
 
-    def edges(at):
+    half = channels // 2 if channels % 256 == 0 else channels
+    for start in range(0, channels, half):
+        at = pl.ds(start, half)
         convolve(0, edge_rows, at)
-        convolve(total - edge_rows, edge_rows, at)
-
-    each_lanes(edges)
+        convolve(total - edge_rows, edge_rows, at, 4 * edge_rows)
     gated_copy = pltpu.make_async_copy(gated, gated_hbm, small_sem.at[3])
     gated_copy.start()
 

time: 46.9 us -> 46.4 us (0.989)
  Pallas kernels: 42.1 us -> 41.6 us
    pallas_call x1, Pallas kernels: 42.1 us -> 41.6 us  [local(): pl.pallas_call(functools.partial(kernel, n, n_ctx), out_shape=(jax.ShapeD...]
where the time goes in v8:
time: 46.4 us; the launch traced here: 45.5 us
  Pallas kernels  41.6 us (90%)
  local copies, waits for them, and re-layouts  3.2 us (7%)
  between operations  0.64 us (1%)
    pallas_call x1, Pallas kernels, local(): pl.pallas_call(functools.partial(kernel, n, n_ctx), out_shape=(jax.ShapeD...  41.6 us
    unnamed x2, local copies, waits for them, and re-layouts  3.2 us

profile of v8, /device:TPU:4, one launch (start us, length us, event | category | flops | bytes accessed | tf_op | source)
XLA Modules:
  0.0 45.5 jit_solution(13843192752990065244)
XLA Ops:
  0.6 41.6 %shard_map.68 = (bf16[96,768]{1,0:T(8,128)(2,1)}, bf16[24,4096]{1,0:T(8,128)(2,1)}) custom-call(bf16[24,4096]{1,0:T(8,128)(2,1)} %tokens.1, bf16[3,4096,768]{2,1,0:T(8,128)(2,1)} %bitcast.1, f32[3,3,768]{2,1,0:T(4,128)} %feat_hbm.1, f32[7,768]{1,0:T(8,128)} %inner_hbm.1, bf16[96,768]{1,0:T(8,128)(2,1)} %grad_hbm.1), custom_call_target="tpu_custom_call" | custom-call | flops 3623878656 | bytes 18874368 | tf_op jit(solution)/shard_map/pallas_call | solution.py:458
  42.3 1.6 %copy.9 = bf16[96,768]{1,0:T(8,128)(2,1)} copy(bf16[96,768]{1,0:T(8,128)(2,1)} %get-tuple-element.4) | data formatting | bytes 294912
  43.9 1.6 %copy.10 = bf16[24,4096]{1,0:T(8,128)(2,1)} copy(bf16[24,4096]{1,0:T(8,128)(2,1)} %get-tuple-element.5) | data formatting | bytes 393216

commit v9 on v8

--- a/solution.py
+++ b/solution.py
@@ -11,7 +11,7 @@
 F32 = jnp.float32
 BF16 = jnp.bfloat16
 PIECES = 8
-GROUPS = ((0, 1), (2, 3), (4, 5), (6,), (7,))
+GROUPS = ((0,), (1,), (2, 3), (4, 5), (6,), (7,))
 HALO = 8
 
 

time: 46.4 us -> 46.4 us (level)
  no operation moved by 1% of the time
where the time goes in v9:
time: 46.4 us; the launch traced here: 45.5 us
  Pallas kernels  41.6 us (90%)
  local copies, waits for them, and re-layouts  3.2 us (7%)
  between operations  0.64 us (1%)
    pallas_call x1, Pallas kernels, local(): pl.pallas_call(functools.partial(kernel, n, n_ctx), out_shape=(jax.ShapeD...  41.6 us
    unnamed x2, local copies, waits for them, and re-layouts  3.2 us

profile of v9, /device:TPU:4, one launch (start us, length us, event | category | flops | bytes accessed | tf_op | source)
XLA Modules:
  0.0 45.5 jit_solution(7368258473059514848)
XLA Ops:
  0.6 41.6 %shard_map.68 = (bf16[96,768]{1,0:T(8,128)(2,1)}, bf16[24,4096]{1,0:T(8,128)(2,1)}) custom-call(bf16[24,4096]{1,0:T(8,128)(2,1)} %tokens.1, bf16[3,4096,768]{2,1,0:T(8,128)(2,1)} %bitcast.1, f32[3,3,768]{2,1,0:T(4,128)} %feat_hbm.1, f32[7,768]{1,0:T(8,128)} %inner_hbm.1, bf16[96,768]{1,0:T(8,128)(2,1)} %grad_hbm.1), custom_call_target="tpu_custom_call" | custom-call | flops 3623878656 | bytes 18874368 | tf_op jit(solution)/shard_map/pallas_call | solution.py:458
  42.3 1.6 %copy.9 = bf16[96,768]{1,0:T(8,128)(2,1)} copy(bf16[96,768]{1,0:T(8,128)(2,1)} %get-tuple-element.4) | data formatting | bytes 294912
  43.9 1.6 %copy.10 = bf16[24,4096]{1,0:T(8,128)(2,1)} copy(bf16[24,4096]{1,0:T(8,128)(2,1)} %get-tuple-element.5) | data formatting | bytes 393216
